TPU v7x, 32 devices: a whole 2x2x4 slice. The times are simulated.
32 devices in a mesh: chrom: 16 (over z, y, x), chan: 2 (over core).
Axes of the slice: x: 2, y: 2, z: 4, core: 2. Of those that a mesh axis runs over, the one named last changes fastest.
Arguments:
- left_embed: bfloat16 [256, 256], P('chrom', 'chan'), may hold values from -6 to 6
- right_embed: bfloat16 [256, 256], P('chrom', 'chan'), may hold values from -6 to 6
- conv_weight: bfloat16 [3, 3, 3, 256, 256], P(None, None, None, None, 'chan'), may hold values from -0.125 to 0.125
- readout: float32 [256], P('chan'), may hold values from -0.375 to 0.375
- cotangent: float32 [256, 64], P('chrom'), may hold values from -6 to 6
Outputs:
- contact: float32 [256, 64], P('chrom')
- left_grad: float32 [256, 256], P('chrom', 'chan')
- right_grad: float32 [256, 256], P('chrom', 'chan')
All inputs are finite; a program needn't handle non-finite values.
Results may differ from a plain program's by a relative error of at most 0.013.
Values may be sent and summed in bfloat16 or wider, within the bound.
A program may use at most 64 MiB of HBM per device.

v0:
```python
import jax
import jax.numpy as jnp
from jax import lax
from jax.sharding import PartitionSpec as P


def passed_along(value, axis, steps):
    count = lax.axis_size(axis)
    initial, last = (max(0, -steps), min(count, count - steps))
    return lax.ppermute(value, axis, [(source, source + steps) for source in range(initial, last)])


def padded_2(array, sides, width):
    for axis, dim in sides:
        devices, length = (lax.axis_size(axis), array.shape[dim])
        up = [(i, (i + 1) % devices) for i in range(devices - 1)]
        down = [(j, i) for i, j in up]
        last = lax.slice_in_dim(array, length - width, length, axis=dim)
        initial = lax.slice_in_dim(array, 0, width, axis=dim)
        before = lax.ppermute(last, axis, up)
        after = lax.ppermute(initial, axis, down)
        array = jnp.concatenate([before, array, after], axis=dim)
    return array


def silu_grad(z):
    s = jax.nn.sigmoid(z)
    return s * (1.0 + z * (1.0 - s))


def local(left_embed, right_embed, conv_weight, readout, cotangent):
    rows, share = left_embed.shape
    band = cotangent.shape[1]
    slabs = band // rows
    layers = conv_weight.shape[0]
    channels = conv_weight.shape[3]

    def pass_along(carry, unused):
        moved = passed_along(carry, "chrom", -1)
        return (moved, moved)

    unused_last, later = lax.scan(pass_along, right_embed, None, length=slabs)
    right_band = jnp.concatenate([right_embed[None], later], axis=0).reshape(-1, share)
    left_wide = left_embed.astype(jnp.float32)
    pair = jnp.stack(
        [
            left_wide[row][None, :] + right_band[row : row + band].astype(jnp.float32)
            for row in range(rows)
        ]
    ).astype(jnp.bfloat16)
    states = []
    for layer in range(layers):
        r = 2**layer
        rimmed = padded_2(pair, (("chrom", 0),), r)
        full = lax.all_gather(rimmed, "chan", axis=2, tiled=True)
        padded = jnp.pad(full, ((0, 0), (r, r), (0, 0)))
        pre = jnp.zeros((rows, band, share), jnp.float32)
        for a in range(3):
            for b in range(3):
                piece = padded[a * r : a * r + rows, b * r : b * r + band, :]
                pre = pre + jnp.dot(
                    piece, conv_weight[layer, a, b], preferred_element_type=jnp.float32
                )
        states.append(pre)
        pair = (pair.astype(jnp.float32) + jax.nn.silu(pre)).astype(jnp.bfloat16)
    contact = lax.psum(jnp.sum(pair.astype(jnp.float32) * readout[None, None, :], axis=-1), "chan")
    grad = cotangent[:, :, None] * readout[None, None, :]
    for layer in reversed(range(layers)):
        r = 2**layer
        dpre = (grad * silu_grad(states[layer])).astype(jnp.bfloat16)
        rimmed = padded_2(dpre, (("chrom", 0),), r)
        padded = jnp.pad(rimmed, ((0, 0), (r, r), (0, 0)))
        part = jnp.zeros((rows, band, channels), jnp.float32)
        for a in range(3):
            for b in range(3):
                piece = padded[
                    (2 - a) * r : (2 - a) * r + rows, (2 - b) * r : (2 - b) * r + band, :
                ]
                part = part + jnp.einsum(
                    "xyo,io->xyi",
                    piece,
                    conv_weight[layer, a, b],
                    preferred_element_type=jnp.float32,
                )
        grad = grad + lax.psum_scatter(
            part.astype(jnp.bfloat16), "chan", scatter_dimension=2, tiled=True
        ).astype(jnp.float32)
    left_grad = jnp.sum(grad, axis=1)
    spread = jnp.zeros((band + rows, share), jnp.float32)
    for row in range(rows):
        spread = spread.at[row : row + band].add(grad[row])
    blocks = spread.reshape(slabs + 1, rows, share)

    def carry_terms(carry, block):
        moved = passed_along(carry + block, "chrom", 1)
        return (moved, None)

    arrived, unused_out = lax.scan(
        carry_terms, jnp.zeros((rows, share), jnp.float32), blocks[1:][::-1]
    )
    right_grad = blocks[0] + arrived
    return (contact, left_grad, right_grad)


def solution(mesh):
    return jax.shard_map(
        local,
        mesh=mesh,
        in_specs=(
            P("chrom", "chan"),
            P("chrom", "chan"),
            P(None, None, None, None, "chan"),
            P("chan"),
            P("chrom", None),
        ),
        out_specs=(P("chrom", None), P("chrom", "chan"), P("chrom", "chan")),
        check_vma=False,
    )
```

profile of v0, /device:TPU:8, one launch (start us, length us, event | category | flops | bytes accessed | tf_op | source)
XLA Modules:
  0.0 210.1 jit_solution(8034450487751861690)
XLA Ops:
  8.0 27.4 %while.38 = (s32[]{:T(128)}, bf16[16,128]{1,0:T(8,128)(2,1)S(1)}, bf16[4,16,128]{2,1,0:T(8,128)(2,1)S(1)}, s32[]{:T(128)}) while((s32[]{:T(128)}, bf16[16,128]{1,0:T(8,128)(2,1)S(1)}, bf16[4,16,128]{2,1,0:T(8,128)(2,1)S(1)}, s32[]{:T(128)}) %tuple.125), condition=%wide.region_1.2_spmd, body=%wide.region_0.1_spmd.sunk | while | flops 2 | bytes 32873 | solution.py:42
  8.0 4.2 %collective-permute-start = (bf16[16,128]{1,0:T(8,128)(2,1)S(1)}, bf16[16,128]{1,0:T(8,128)(2,1)S(1)}, u32[]{:S(2)}, u32[]{:S(2)}) collective-permute-start(bf16[16,128]{1,0:T(8,128)(2,1)S(1)} %get-tuple-element.324), channel_id=1, source_target_pairs={{2,0},{4,2},{6,4},{8,6},{10,8},{12,10},{14,12},{16,14},{18,16},{20... | collective-permute-start | bytes 12296 | tf_op jit(solution)/shard_map/while/body/eval_jaxpr/ppermute | solution.py:10
  13.6 6.0 %collective-permute-start = (bf16[16,128]{1,0:T(8,128)(2,1)S(1)}, bf16[16,128]{1,0:T(8,128)(2,1)S(1)}, u32[]{:S(2)}, u32[]{:S(2)}) collective-permute-start(bf16[16,128]{1,0:T(8,128)(2,1)S(1)} %get-tuple-element.324), channel_id=1, source_target_pairs={{2,0},{4,2},{6,4},{8,6},{10,8},{12,10},{14,12},{16,14},{18,16},{20... | collective-permute-start | bytes 12296 | tf_op jit(solution)/shard_map/while/body/eval_jaxpr/ppermute | solution.py:10
  20.9 6.0 %collective-permute-start = (bf16[16,128]{1,0:T(8,128)(2,1)S(1)}, bf16[16,128]{1,0:T(8,128)(2,1)S(1)}, u32[]{:S(2)}, u32[]{:S(2)}) collective-permute-start(bf16[16,128]{1,0:T(8,128)(2,1)S(1)} %get-tuple-element.324), channel_id=1, source_target_pairs={{2,0},{4,2},{6,4},{8,6},{10,8},{12,10},{14,12},{16,14},{18,16},{20... | collective-permute-start | bytes 12296 | tf_op jit(solution)/shard_map/while/body/eval_jaxpr/ppermute | solution.py:10
  28.2 6.0 %collective-permute-start = (bf16[16,128]{1,0:T(8,128)(2,1)S(1)}, bf16[16,128]{1,0:T(8,128)(2,1)S(1)}, u32[]{:S(2)}, u32[]{:S(2)}) collective-permute-start(bf16[16,128]{1,0:T(8,128)(2,1)S(1)} %get-tuple-element.324), channel_id=1, source_target_pairs={{2,0},{4,2},{6,4},{8,6},{10,8},{12,10},{14,12},{16,14},{18,16},{20... | collective-permute-start | bytes 12296 | tf_op jit(solution)/shard_map/while/body/eval_jaxpr/ppermute | solution.py:10
  39.8 6.0 %collective-permute-start.3 = (bf16[1,64,128]{2,1,0:T(8,128)(2,1)S(1)}, bf16[1,64,128]{2,1,0:T(8,128)(2,1)S(1)}, u32[]{:S(2)}, u32[]{:S(2)}) collective-permute-start(bf16[1,64,128]{2,1,0:T(8,128)(2,1)S(1)} %get-tuple-element.248), channel_id=1, source_target_pairs={{2,0},{4,2},{6,4},{8,6},{10,8},{12,10},{14,12},{16,14},{18,16},{20... | collective-permute-start | bytes 49160 | tf_op jit(solution)/shard_map/ppermute | solution.py:21
  53.1 4.3 %collective-permute-start.4 = (bf16[2,64,128]{2,1,0:T(8,128)(2,1)S(1)}, bf16[2,64,128]{2,1,0:T(8,128)(2,1)S(1)}, u32[]{:S(2)}, u32[]{:S(2)}) collective-permute-start(bf16[2,64,128]{2,1,0:T(8,128)(2,1)S(1)} %get-tuple-element.259), channel_id=1, source_target_pairs={{0,2},{2,4},{4,6},{6,8},{8,10},{10,12},{12,14},{14,16},{16,18},{18... | collective-permute-start | bytes 98312 | tf_op jit(solution)/shard_map/ppermute | solution.py:20
  57.4 3.6 %collective-permute-start.5 = (bf16[2,64,128]{2,1,0:T(8,128)(2,1)S(1)}, bf16[2,64,128]{2,1,0:T(8,128)(2,1)S(1)}, u32[]{:S(2)}, u32[]{:S(2)}) collective-permute-start(bf16[2,64,128]{2,1,0:T(8,128)(2,1)S(1)} %get-tuple-element.260), channel_id=1, source_target_pairs={{2,0},{4,2},{6,4},{8,6},{10,8},{12,10},{14,12},{16,14},{18,16},{20... | collective-permute-start | bytes 98312 | tf_op jit(solution)/shard_map/ppermute | solution.py:21
  69.3 4.8 %collective-permute-start.6 = (bf16[4,64,128]{2,1,0:T(8,128)(2,1)S(1)}, bf16[4,64,128]{2,1,0:T(8,128)(2,1)S(1)}, u32[]{:S(2)}, u32[]{:S(2)}) collective-permute-start(bf16[4,64,128]{2,1,0:T(8,128)(2,1)S(1)} %get-tuple-element.257), channel_id=1, source_target_pairs={{0,2},{2,4},{4,6},{6,8},{8,10},{10,12},{12,14},{14,16},{16,18},{18... | collective-permute-start | bytes 196616 | tf_op jit(solution)/shard_map/ppermute | solution.py:20
  86.1 4.6 %collective-permute-start.9 = (bf16[4,64,128]{2,1,0:T(8,128)(2,1)S(1)}, bf16[4,64,128]{2,1,0:T(8,128)(2,1)S(1)}, u32[]{:S(2)}, u32[]{:S(2)}) collective-permute-start(bf16[4,64,128]{2,1,0:T(8,128)(2,1)S(1)} %get-tuple-element.256), channel_id=1, source_target_pairs={{2,0},{4,2},{6,4},{8,6},{10,8},{12,10},{14,12},{16,14},{18,16},{20... | collective-permute-start | bytes 196616 | tf_op jit(solution)/shard_map/ppermute | solution.py:21
  92.7 6.0 %collective-permute-done.8 = bf16[4,64,128]{2,1,0:T(8,128)(2,1)S(1)} collective-permute-done((bf16[4,64,128]{2,1,0:T(8,128)(2,1)S(1)}, bf16[4,64,128]{2,1,0:T(8,128)(2,1)S(1)}, u32[]{:S(2)}, u32[]{:S(2)}) %collective-permute-start.8) | collective-permute-done | bytes 65568 | tf_op jit(solution)/shard_map/ppermute | solution.py:20
  104.3 7.1 %reduce-scatter.10.cloned.1.call-done = bf16[128,1024]{1,0:T(8,128)(2,1)} async-done(((bf16[256,1024]{1,0:T(8,128)(2,1)}), bf16[128,1024]{1,0:T(8,128)(2,1)}) %reduce-scatter.10.cloned.1.call-update) | async-done | bytes 262160
  113.5 4.3 %collective-permute-start.11 = (bf16[2,64,128]{2,1,0:T(8,128)(2,1)S(1)}, bf16[2,64,128]{2,1,0:T(8,128)(2,1)S(1)}, u32[]{:S(2)}, u32[]{:S(2)}) collective-permute-start(bf16[2,64,128]{2,1,0:T(8,128)(2,1)S(1)} %get-tuple-element.254), channel_id=1, source_target_pairs={{2,0},{4,2},{6,4},{8,6},{10,8},{12,10},{14,12},{16,14},{18,16},{20... | collective-permute-start | bytes 98312 | tf_op jit(solution)/shard_map/ppermute | solution.py:21
  119.7 5.7 %collective-permute-done.10 = bf16[2,64,128]{2,1,0:T(8,128)(2,1)S(1)} collective-permute-done((bf16[2,64,128]{2,1,0:T(8,128)(2,1)S(1)}, bf16[2,64,128]{2,1,0:T(8,128)(2,1)S(1)}, u32[]{:S(2)}, u32[]{:S(2)}) %collective-permute-start.10) | collective-permute-done | bytes 32800 | tf_op jit(solution)/shard_map/ppermute | solution.py:20
  132.7 7.4 %reduce-scatter.12.cloned.1.call-done = bf16[128,1024]{1,0:T(8,128)(2,1)} async-done(((bf16[256,1024]{1,0:T(8,128)(2,1)}), bf16[128,1024]{1,0:T(8,128)(2,1)}) %reduce-scatter.12.cloned.1.call-update) | async-done | bytes 262160
  142.2 4.3 %collective-permute-start.13 = (bf16[1,64,128]{2,1,0:T(8,128)(2,1)S(1)}, bf16[1,64,128]{2,1,0:T(8,128)(2,1)S(1)}, u32[]{:S(2)}, u32[]{:S(2)}) collective-permute-start(bf16[1,64,128]{2,1,0:T(8,128)(2,1)S(1)} %get-tuple-element.252), channel_id=1, source_target_pairs={{2,0},{4,2},{6,4},{8,6},{10,8},{12,10},{14,12},{16,14},{18,16},{20... | collective-permute-start | bytes 49160 | tf_op jit(solution)/shard_map/ppermute | solution.py:21
  148.4 5.5 %collective-permute-done.12 = bf16[1,64,128]{2,1,0:T(8,128)(2,1)S(1)} collective-permute-done((bf16[1,64,128]{2,1,0:T(8,128)(2,1)S(1)}, bf16[1,64,128]{2,1,0:T(8,128)(2,1)S(1)}, u32[]{:S(2)}, u32[]{:S(2)}) %collective-permute-start.12) | collective-permute-done | bytes 16416 | tf_op jit(solution)/shard_map/ppermute | solution.py:20
  162.4 4.3 %reduce-scatter.14.cloned.1.call-done = bf16[128,1024]{1,0:T(8,128)(2,1)} async-done(((bf16[256,1024]{1,0:T(8,128)(2,1)}), bf16[128,1024]{1,0:T(8,128)(2,1)}) %reduce-scatter.14.cloned.1.call-update) | async-done | bytes 262160
  173.6 29.4 %while.39 = (s32[]{:T(128)}, f32[16,128]{1,0:T(8,128)S(1)}, f32[4,16,128]{2,1,0:T(8,128)S(1)}, s32[]{:T(128)}) while((s32[]{:T(128)}, f32[16,128]{1,0:T(8,128)S(1)}, f32[4,16,128]{2,1,0:T(8,128)S(1)}, s32[]{:T(128)}) %tuple.128), condition=%wide.region_9.10_spmd, body=%wide.region_8.9_spmd.sunk | while | flops 2050 | bytes 57441 | solution.py:98
  173.6 3.4 %collective-permute-start.1 = (f32[16,128]{1,0:T(8,128)S(1)}, f32[16,128]{1,0:T(8,128)S(1)}, u32[]{:S(2)}, u32[]{:S(2)}) collective-permute-start(f32[16,128]{1,0:T(8,128)S(1)} %bitcast_add_fusion.2), channel_id=1, source_target_pairs={{0,2},{2,4},{4,6},{6,8},{8,10},{10,12},{12,14},{14,16},{16,18},{18... | collective-permute-start | bytes 24584 | tf_op jit(solution)/shard_map/while/body/eval_jaxpr/ppermute | solution.py:10
  177.0 3.9 %collective-permute-done.1 = f32[16,128]{1,0:T(8,128)S(1)} collective-permute-done((f32[16,128]{1,0:T(8,128)S(1)}, f32[16,128]{1,0:T(8,128)S(1)}, u32[]{:S(2)}, u32[]{:S(2)}) %collective-permute-start.1) | collective-permute-done | bytes 8224 | tf_op jit(solution)/shard_map/while/body/eval_jaxpr/ppermute | solution.py:10
  182.8 5.4 %collective-permute-done.1 = f32[16,128]{1,0:T(8,128)S(1)} collective-permute-done((f32[16,128]{1,0:T(8,128)S(1)}, f32[16,128]{1,0:T(8,128)S(1)}, u32[]{:S(2)}, u32[]{:S(2)}) %collective-permute-start.1) | collective-permute-done | bytes 8224 | tf_op jit(solution)/shard_map/while/body/eval_jaxpr/ppermute | solution.py:10
  190.2 5.4 %collective-permute-done.1 = f32[16,128]{1,0:T(8,128)S(1)} collective-permute-done((f32[16,128]{1,0:T(8,128)S(1)}, f32[16,128]{1,0:T(8,128)S(1)}, u32[]{:S(2)}, u32[]{:S(2)}) %collective-permute-start.1) | collective-permute-done | bytes 8224 | tf_op jit(solution)/shard_map/while/body/eval_jaxpr/ppermute | solution.py:10
  197.5 5.4 %collective-permute-done.1 = f32[16,128]{1,0:T(8,128)S(1)} collective-permute-done((f32[16,128]{1,0:T(8,128)S(1)}, f32[16,128]{1,0:T(8,128)S(1)}, u32[]{:S(2)}, u32[]{:S(2)}) %collective-permute-start.1) | collective-permute-done | bytes 8224 | tf_op jit(solution)/shard_map/while/body/eval_jaxpr/ppermute | solution.py:10
  (207 shorter events, 81.6 us)
Async XLA Ops:
  7.2 42.3 %copy-start = (bf16[3,3,3,256,128]{4,3,2,1,0:T(8,128)(2,1)S(1)}, bf16[3,3,3,256,128]{4,3,2,1,0:T(8,128)(2,1)}, u32[]{:S(2)}) copy-start(bf16[3,3,3,256,128]{4,3,2,1,0:T(8,128)(2,1)} %param.43) | copy-start | bytes 5308420
  7.2 104.2 %reduce-scatter.10.cloned.1.call-start = ((), (), s32[]{:S(2)}) async-start(), calls=%async_computation.3 | async-start | bytes 786432
  8.0 5.5 %collective-permute-start = (bf16[16,128]{1,0:T(8,128)(2,1)S(1)}, bf16[16,128]{1,0:T(8,128)(2,1)S(1)}, u32[]{:S(2)}, u32[]{:S(2)}) collective-permute-start(bf16[16,128]{1,0:T(8,128)(2,1)S(1)} %get-tuple-element.324), channel_id=1, source_target_pairs={{2,0},{4,2},{6,4},{8,6},{10,8},{12,10},{14,12},{16,14},{18,16},{20... | collective-permute-start | bytes 12296 | tf_op jit(solution)/shard_map/while/body/eval_jaxpr/ppermute | solution.py:10
  13.6 7.3 %collective-permute-start = (bf16[16,128]{1,0:T(8,128)(2,1)S(1)}, bf16[16,128]{1,0:T(8,128)(2,1)S(1)}, u32[]{:S(2)}, u32[]{:S(2)}) collective-permute-start(bf16[16,128]{1,0:T(8,128)(2,1)S(1)} %get-tuple-element.324), channel_id=1, source_target_pairs={{2,0},{4,2},{6,4},{8,6},{10,8},{12,10},{14,12},{16,14},{18,16},{20... | collective-permute-start | bytes 12296 | tf_op jit(solution)/shard_map/while/body/eval_jaxpr/ppermute | solution.py:10
  20.9 7.3 %collective-permute-start = (bf16[16,128]{1,0:T(8,128)(2,1)S(1)}, bf16[16,128]{1,0:T(8,128)(2,1)S(1)}, u32[]{:S(2)}, u32[]{:S(2)}) collective-permute-start(bf16[16,128]{1,0:T(8,128)(2,1)S(1)} %get-tuple-element.324), channel_id=1, source_target_pairs={{2,0},{4,2},{6,4},{8,6},{10,8},{12,10},{14,12},{16,14},{18,16},{20... | collective-permute-start | bytes 12296 | tf_op jit(solution)/shard_map/while/body/eval_jaxpr/ppermute | solution.py:10
  28.2 7.3 %collective-permute-start = (bf16[16,128]{1,0:T(8,128)(2,1)S(1)}, bf16[16,128]{1,0:T(8,128)(2,1)S(1)}, u32[]{:S(2)}, u32[]{:S(2)}) collective-permute-start(bf16[16,128]{1,0:T(8,128)(2,1)S(1)} %get-tuple-element.324), channel_id=1, source_target_pairs={{2,0},{4,2},{6,4},{8,6},{10,8},{12,10},{14,12},{16,14},{18,16},{20... | collective-permute-start | bytes 12296 | tf_op jit(solution)/shard_map/while/body/eval_jaxpr/ppermute | solution.py:10
  37.9 7.9 %collective-permute-start.2 = (bf16[1,64,128]{2,1,0:T(8,128)(2,1)S(1)}, bf16[1,64,128]{2,1,0:T(8,128)(2,1)S(1)}, u32[]{:S(2)}, u32[]{:S(2)}) collective-permute-start(bf16[1,64,128]{2,1,0:T(8,128)(2,1)S(1)} %get-tuple-element.246), channel_id=1, source_target_pairs={{0,2},{2,4},{4,6},{6,8},{8,10},{10,12},{12,14},{14,16},{16,18},{18... | collective-permute-start | bytes 49160 | tf_op jit(solution)/shard_map/ppermute | solution.py:20
  39.8 7.4 %collective-permute-start.3 = (bf16[1,64,128]{2,1,0:T(8,128)(2,1)S(1)}, bf16[1,64,128]{2,1,0:T(8,128)(2,1)S(1)}, u32[]{:S(2)}, u32[]{:S(2)}) collective-permute-start(bf16[1,64,128]{2,1,0:T(8,128)(2,1)S(1)} %get-tuple-element.248), channel_id=1, source_target_pairs={{2,0},{4,2},{6,4},{8,6},{10,8},{12,10},{14,12},{16,14},{18,16},{20... | collective-permute-start | bytes 49160 | tf_op jit(solution)/shard_map/ppermute | solution.py:21
  53.1 7.9 %collective-permute-start.4 = (bf16[2,64,128]{2,1,0:T(8,128)(2,1)S(1)}, bf16[2,64,128]{2,1,0:T(8,128)(2,1)S(1)}, u32[]{:S(2)}, u32[]{:S(2)}) collective-permute-start(bf16[2,64,128]{2,1,0:T(8,128)(2,1)S(1)} %get-tuple-element.259), channel_id=1, source_target_pairs={{0,2},{2,4},{4,6},{6,8},{8,10},{10,12},{12,14},{14,16},{16,18},{18... | collective-permute-start | bytes 98312 | tf_op jit(solution)/shard_map/ppermute | solution.py:20
  57.4 5.8 %collective-permute-start.5 = (bf16[2,64,128]{2,1,0:T(8,128)(2,1)S(1)}, bf16[2,64,128]{2,1,0:T(8,128)(2,1)S(1)}, u32[]{:S(2)}, u32[]{:S(2)}) collective-permute-start(bf16[2,64,128]{2,1,0:T(8,128)(2,1)S(1)} %get-tuple-element.260), channel_id=1, source_target_pairs={{2,0},{4,2},{6,4},{8,6},{10,8},{12,10},{14,12},{16,14},{18,16},{20... | collective-permute-start | bytes 98312 | tf_op jit(solution)/shard_map/ppermute | solution.py:21
  69.3 8.0 %collective-permute-start.6 = (bf16[4,64,128]{2,1,0:T(8,128)(2,1)S(1)}, bf16[4,64,128]{2,1,0:T(8,128)(2,1)S(1)}, u32[]{:S(2)}, u32[]{:S(2)}) collective-permute-start(bf16[4,64,128]{2,1,0:T(8,128)(2,1)S(1)} %get-tuple-element.257), channel_id=1, source_target_pairs={{0,2},{2,4},{4,6},{6,8},{8,10},{10,12},{12,14},{14,16},{16,18},{18... | collective-permute-start | bytes 196616 | tf_op jit(solution)/shard_map/ppermute | solution.py:20
  74.1 6.2 %collective-permute-start.7 = (bf16[4,64,128]{2,1,0:T(8,128)(2,1)S(1)}, bf16[4,64,128]{2,1,0:T(8,128)(2,1)S(1)}, u32[]{:S(2)}, u32[]{:S(2)}) collective-permute-start(bf16[4,64,128]{2,1,0:T(8,128)(2,1)S(1)} %get-tuple-element.258), channel_id=1, source_target_pairs={{2,0},{4,2},{6,4},{8,6},{10,8},{12,10},{14,12},{16,14},{18,16},{20... | collective-permute-start | bytes 196616 | tf_op jit(solution)/shard_map/ppermute | solution.py:21
  86.1 6.6 %collective-permute-start.9 = (bf16[4,64,128]{2,1,0:T(8,128)(2,1)S(1)}, bf16[4,64,128]{2,1,0:T(8,128)(2,1)S(1)}, u32[]{:S(2)}, u32[]{:S(2)}) collective-permute-start(bf16[4,64,128]{2,1,0:T(8,128)(2,1)S(1)} %get-tuple-element.256), channel_id=1, source_target_pairs={{2,0},{4,2},{6,4},{8,6},{10,8},{12,10},{14,12},{16,14},{18,16},{20... | collective-permute-start | bytes 196616 | tf_op jit(solution)/shard_map/ppermute | solution.py:21
  90.8 8.0 %collective-permute-start.8 = (bf16[4,64,128]{2,1,0:T(8,128)(2,1)S(1)}, bf16[4,64,128]{2,1,0:T(8,128)(2,1)S(1)}, u32[]{:S(2)}, u32[]{:S(2)}) collective-permute-start(bf16[4,64,128]{2,1,0:T(8,128)(2,1)S(1)} %get-tuple-element.255), channel_id=1, source_target_pairs={{0,2},{2,4},{4,6},{6,8},{8,10},{10,12},{12,14},{14,16},{16,18},{18... | collective-permute-start | bytes 196616 | tf_op jit(solution)/shard_map/ppermute | solution.py:20
  104.1 36.0 %reduce-scatter.12.cloned.1.call-start = ((), (), s32[]{:S(2)}) async-start(), calls=%async_computation.4 | async-start | bytes 786432
  113.5 6.2 %collective-permute-start.11 = (bf16[2,64,128]{2,1,0:T(8,128)(2,1)S(1)}, bf16[2,64,128]{2,1,0:T(8,128)(2,1)S(1)}, u32[]{:S(2)}, u32[]{:S(2)}) collective-permute-start(bf16[2,64,128]{2,1,0:T(8,128)(2,1)S(1)} %get-tuple-element.254), channel_id=1, source_target_pairs={{2,0},{4,2},{6,4},{8,6},{10,8},{12,10},{14,12},{16,14},{18,16},{20... | collective-permute-start | bytes 98312 | tf_op jit(solution)/shard_map/ppermute | solution.py:21
  117.8 7.6 %collective-permute-start.10 = (bf16[2,64,128]{2,1,0:T(8,128)(2,1)S(1)}, bf16[2,64,128]{2,1,0:T(8,128)(2,1)S(1)}, u32[]{:S(2)}, u32[]{:S(2)}) collective-permute-start(bf16[2,64,128]{2,1,0:T(8,128)(2,1)S(1)} %get-tuple-element.253), channel_id=1, source_target_pairs={{0,2},{2,4},{4,6},{6,8},{8,10},{10,12},{12,14},{14,16},{16,18},{18... | collective-permute-start | bytes 98312 | tf_op jit(solution)/shard_map/ppermute | solution.py:20
  132.6 34.1 %reduce-scatter.14.cloned.1.call-start = ((), (), s32[]{:S(2)}) async-start(), calls=%async_computation.5 | async-start | bytes 786432
  142.2 6.2 %collective-permute-start.13 = (bf16[1,64,128]{2,1,0:T(8,128)(2,1)S(1)}, bf16[1,64,128]{2,1,0:T(8,128)(2,1)S(1)}, u32[]{:S(2)}, u32[]{:S(2)}) collective-permute-start(bf16[1,64,128]{2,1,0:T(8,128)(2,1)S(1)} %get-tuple-element.252), channel_id=1, source_target_pairs={{2,0},{4,2},{6,4},{8,6},{10,8},{12,10},{14,12},{16,14},{18,16},{20... | collective-permute-start | bytes 49160 | tf_op jit(solution)/shard_map/ppermute | solution.py:21
  146.5 7.4 %collective-permute-start.12 = (bf16[1,64,128]{2,1,0:T(8,128)(2,1)S(1)}, bf16[1,64,128]{2,1,0:T(8,128)(2,1)S(1)}, u32[]{:S(2)}, u32[]{:S(2)}) collective-permute-start(bf16[1,64,128]{2,1,0:T(8,128)(2,1)S(1)} %get-tuple-element.251), channel_id=1, source_target_pairs={{0,2},{2,4},{4,6},{6,8},{8,10},{10,12},{12,14},{14,16},{16,18},{18... | collective-permute-start | bytes 49160 | tf_op jit(solution)/shard_map/ppermute | solution.py:20
  173.6 7.3 %collective-permute-start.1 = (f32[16,128]{1,0:T(8,128)S(1)}, f32[16,128]{1,0:T(8,128)S(1)}, u32[]{:S(2)}, u32[]{:S(2)}) collective-permute-start(f32[16,128]{1,0:T(8,128)S(1)} %bitcast_add_fusion.2), channel_id=1, source_target_pairs={{0,2},{2,4},{4,6},{6,8},{8,10},{10,12},{12,14},{14,16},{16,18},{18... | collective-permute-start | bytes 24584 | tf_op jit(solution)/shard_map/while/body/eval_jaxpr/ppermute | solution.py:10
  180.9 7.3 %collective-permute-start.1 = (f32[16,128]{1,0:T(8,128)S(1)}, f32[16,128]{1,0:T(8,128)S(1)}, u32[]{:S(2)}, u32[]{:S(2)}) collective-permute-start(f32[16,128]{1,0:T(8,128)S(1)} %bitcast_add_fusion.2), channel_id=1, source_target_pairs={{0,2},{2,4},{4,6},{6,8},{8,10},{10,12},{12,14},{14,16},{16,18},{18... | collective-permute-start | bytes 24584 | tf_op jit(solution)/shard_map/while/body/eval_jaxpr/ppermute | solution.py:10
  188.3 7.3 %collective-permute-start.1 = (f32[16,128]{1,0:T(8,128)S(1)}, f32[16,128]{1,0:T(8,128)S(1)}, u32[]{:S(2)}, u32[]{:S(2)}) collective-permute-start(f32[16,128]{1,0:T(8,128)S(1)} %bitcast_add_fusion.2), channel_id=1, source_target_pairs={{0,2},{2,4},{4,6},{6,8},{8,10},{10,12},{12,14},{14,16},{16,18},{18... | collective-permute-start | bytes 24584 | tf_op jit(solution)/shard_map/while/body/eval_jaxpr/ppermute | solution.py:10
  195.6 7.3 %collective-permute-start.1 = (f32[16,128]{1,0:T(8,128)S(1)}, f32[16,128]{1,0:T(8,128)S(1)}, u32[]{:S(2)}, u32[]{:S(2)}) collective-permute-start(f32[16,128]{1,0:T(8,128)S(1)} %bitcast_add_fusion.2), channel_id=1, source_target_pairs={{0,2},{2,4},{4,6},{6,8},{8,10},{10,12},{12,14},{14,16},{16,18},{18... | collective-permute-start | bytes 24584 | tf_op jit(solution)/shard_map/while/body/eval_jaxpr/ppermute | solution.py:10
  (4 other events, 21.3 us)
Sparse Core Ops, SparseCore 0:
  104.2 7.1 reduce-scatter.9
  132.8 7.2 reduce-scatter.11
  159.4 7.2 reduce-scatter.13
where the time goes:
time: 211 us; the launch traced here: 210 us
  starting transfers between devices  74 us (35%)
  waiting for transfers between devices  68 us (32%)
  matrix products  19.1 us (9%)
  local copies, waits for them, and re-layouts  18.9 us (9%)
  between operations  14.8 us (7%)
  blocking collectives  9.95 us (5%)
  other arithmetic  5.29 us (3%)
    ppermute x8, starting transfers between devices, passed_along(): lax.ppermute(value, axis, [(source, source + steps) for source in range(i...  31.3 us
    ppermute x6, starting transfers between devices, padded_2(): after = lax.ppermute(initial, axis, down)  25.6 us
    ppermute x8, waiting for transfers between devices, passed_along(): lax.ppermute(value, axis, [(source, source + steps) for source in range(i...  25.4 us
    unnamed x6, waiting for transfers between devices  18.8 us
    ppermute x6, waiting for transfers between devices, padded_2(): before = lax.ppermute(last, axis, up)  17.5 us
    ppermute x6, starting transfers between devices, padded_2(): before = lax.ppermute(last, axis, up)  16.8 us
    unnamed x26, local copies, waits for them, and re-layouts  15 us
    dot_general x27, matrix products, local(): jnp.dot(piece, conv_weight[layer, a, b], preferred_element_type=jnp.float32)  10.2 us
  transfers between devices with their start and end apart: 23, of which 18 were waited for; matrix products, arithmetic and copies ran while one was open for 0% of the time, Pallas kernels for 0%

commit v1 on v0

v1 whole, which is shorter than its diff:
```python
import functools

import jax
import jax.numpy as jnp
from jax import lax
from jax.experimental import pallas as pl
from jax.experimental.pallas import tpu as pltpu
from jax.sharding import PartitionSpec as P

MESH = pl.DeviceIdType.MESH
F32, BF16 = jnp.float32, jnp.bfloat16
BACK, AHEAD = 1, 5
Q = 4


def split3(x):
    hi = x.astype(BF16)
    rest = x - hi.astype(F32)
    mid = rest.astype(BF16)
    return hi, mid, (rest - mid.astype(F32)).astype(BF16)


def nt(a, b):
    return lax.dot_general(a, b, (((1,), (1,)), ((), ())), preferred_element_type=F32)


def shifted(x, step):
    n = x.shape[2]
    flat = x.reshape((x.shape[0] * x.shape[1],) + x.shape[2:])
    moved = pltpu.roll(flat, step % n, 1)
    where = lax.broadcasted_iota(jnp.int32, flat.shape, 1)
    edge = 0 if step == 1 else n - 1
    return jnp.where(where == edge, 0.0, moved).reshape(x.shape)


def put(buf, row, x, r):
    rows = pl.ds(row, x.shape[0])
    buf[rows, r : r + Q] = x.astype(BF16)
    buf[rows, 0:r] = shifted(x[:, Q - r :], 1).astype(BF16)
    buf[rows, r + Q :] = shifted(x[:, :r], -1).astype(BF16)


def kernel(
    slabs,
    left_ref, right_ref, w_hbm, ro_ref, cot_ref,
    contact_out, lg_out, rg_out,
    block, emb, rwin, w, cot, ro, p0, p1, p2, d2, d1, d0, s0, s1, g2, g1,
    spread, rg, swap_out, swap,
    emb_ss, emb_rs, w_ls, w_ss, w_rs, cot_ss, cot_rs, ro_ss, ro_rs, rg_ss, rg_rs, swap_ss, swap_rs,
):
    slab = lax.axis_index("chrom")
    half = lax.axis_index("chan")
    mate = 1 - half

    def there(delta):
        return jnp.logical_and(slab + delta >= 0, slab + delta < slabs)

    def send(src, dst, ss, rs, delta, chan):
        return pltpu.make_async_remote_copy(
            src_ref=src, dst_ref=dst, send_sem=ss, recv_sem=rs,
            device_id=(slab + delta, chan), device_id_type=MESH,
        )

    barrier = pltpu.get_barrier_semaphore()
    reach = max(BACK, AHEAD)
    for delta in range(-reach, reach + 1):
        if delta == 0:
            pl.semaphore_signal(barrier, inc=1, device_id=(slab, mate), device_id_type=MESH)
        else:
            @pl.when(there(delta))
            def _(delta=delta):
                for chan in range(2):
                    pl.semaphore_signal(barrier, inc=1, device_id=(slab + delta, chan), device_id_type=MESH)

    layers = w.shape[1]
    local = [pltpu.make_async_copy(w_hbm.at[k], w.at[half, k], w_ls.at[k]) for k in range(layers)]
    for copy in local:
        copy.start()
    block[0:16] = right_ref[...]
    block[16:32] = left_ref[...]
    emb[BACK, half] = block[...]
    cot[16:32] = jnp.concatenate([cot_ref[...], jnp.zeros((16, 64), F32)], axis=1)
    ro[half] = jnp.broadcast_to(ro_ref[...], (8, 128))
    for k in range(BACK + AHEAD + 1):
        if k != BACK:
            @pl.when(jnp.logical_not(there(k - BACK)))
            def _(k=k):
                emb[k] = jnp.zeros(emb.shape[1:], BF16)
    for delta in (-1, 1):
        @pl.when(jnp.logical_not(there(delta)))
        def _(delta=delta):
            cot[16 + 16 * delta : 32 + 16 * delta] = jnp.zeros((16, 128), F32)

    pl.semaphore_wait(
        barrier, 2 * (jnp.minimum(slab, reach) + jnp.minimum(slabs - 1 - slab, reach) + 1) - 1
    )

    def emb_copy(delta, chan):
        k = BACK - delta
        return send(block, emb.at[k, half], emb_ss.at[k, chan], emb_rs.at[k, half], delta, chan)

    def each_emb(act):
        for delta in (0, 1, -1, -2, -3, -4, -5):
            if delta == 0:
                act(emb_copy(0, mate))
            else:
                @pl.when(there(delta))
                def _(delta=delta):
                    for chan in range(2):
                        act(emb_copy(delta, chan))

    def w_copy(k):
        return send(w_hbm.at[k], w.at[half, k], w_ss.at[k], w_rs.at[k], 0, mate)

    def cot_copy(delta):
        place = pl.ds(16 - 16 * delta, 16)
        slot = (1 - delta) // 2
        return send(cot.at[pl.ds(16, 16)], cot.at[place], cot_ss.at[slot], cot_rs.at[slot], delta, half)

    def each_cot(act):
        for delta in (-1, 1):
            @pl.when(there(delta))
            def _(delta=delta):
                act(cot_copy(delta))

    ro_copy = send(ro.at[half], ro.at[half], ro_ss.at[0], ro_rs.at[0], 0, mate)

    each_emb(lambda c: c.start())
    for k in range(layers):
        w_copy(k).start()
    ro_copy.start()
    each_cot(lambda c: c.start())

    def emb_wait(k, chan):
        send(block, emb.at[k, chan], emb_ss.at[k, chan], emb_rs.at[k, chan], 0, mate).wait_recv()

    for k in range(BACK + AHEAD + 1):
        if k == BACK:
            emb_wait(k, mate)
        else:
            @pl.when(there(k - BACK))
            def _(k=k):
                for chan in range(2):
                    emb_wait(k, chan)

    for k in range(BACK + AHEAD + 1):
        for c in range(2):
            rwin[c, 16 * k : 16 * k + 16] = emb[k, c, 0:16].astype(F32)
            if k < 3:
                rwin[2 + c, 16 * k : 16 * k + 16] = emb[k, c, 16:32].astype(F32)
    start = pl.multiple_of(8 * half, 8)
    for c in range(2):
        rwin[c, 0:104] = rwin[c, pl.ds(start, 104)]
    lwin = jnp.concatenate([rwin[2 + c, pl.ds(start, 40)] for c in range(2)], axis=1)

    def clear(buf, first, count):
        for h in range(2):
            low, high = 16 - 8 * h, 32 - 8 * h
            if first < low:
                @pl.when(jnp.logical_and(slab == 0, half == h))
                def _():
                    n = min(low, first + count) - first
                    buf[0:n] = jnp.zeros((n,) + buf.shape[1:], BF16)
            if first + count > high:
                @pl.when(jnp.logical_and(slab == slabs - 1, half == h))
                def _():
                    begin = max(high - first, 0)
                    buf[begin:count] = jnp.zeros((count - begin,) + buf.shape[1:], BF16)

    diag = {}
    for i in range(36):
        tiles = []
        for q in range(Q):
            t = 2 + i + q
            if t not in diag:
                diag[t] = jnp.concatenate([rwin[c, pl.ds(t, 16, stride=Q), :] for c in range(2)], axis=1)
            tiles.append(diag[t] + lwin[2 + i : 3 + i, :])
        put(p0, i, jnp.stack(tiles)[None], 1)
    clear(p0, 2, 36)

    def weights(k):
        local[k].wait()
        send(w_hbm.at[k], w.at[mate, k], w_ss.at[k], w_rs.at[k], 0, mate).wait_recv()

    def forward(k, src, src_first, first, count, chunk, sink):
        r = 2**k
        weights(k)
        wide = jnp.concatenate([w[c, k].reshape(9 * 256, 128) for c in range(2)], axis=1)
        for begin in range(first, first + count, chunk):
            n = min(chunk, first + count - begin)
            lhs = jnp.concatenate(
                [
                    src[pl.ds(begin + (a - 1) * r - src_first, n), b * r : b * r + Q].reshape(n * 64, 256)
                    for a in range(3) for b in range(3)
                ],
                axis=1,
            )
            z = jnp.dot(lhs, wide, preferred_element_type=F32).reshape(n, Q, 16, 256)
            s = 0.5 + 0.5 * jnp.tanh(0.5 * z)
            old = src[pl.ds(begin - src_first, n), r : r + Q].astype(F32)
            zs = z * s
            sink(begin, n, old + zs, s + zs * (1.0 - s))

    def keep(buf, buf_first, r, slopes, slopes_first):
        count = slopes.shape[0]

        def sink(begin, n, x, slope):
            if buf is not None:
                put(buf, begin - buf_first, x, r)
            low, high = max(begin, slopes_first), min(begin + n, slopes_first + count)
            if low < high:
                slopes[pl.ds(low - slopes_first, high - low)] = slope[low - begin : high - begin]

        return sink

    forward(0, p0, 2, 3, 34, 9, keep(p1, 3, 2, s0, 15))
    clear(p1, 3, 34)
    forward(1, p1, 3, 5, 30, 10, keep(p2, 5, 4, s1, 13))
    clear(p2, 5, 30)

    n_i = lax.broadcasted_iota(jnp.int32, (64, 128), 0)
    d_i = lax.broadcasted_iota(jnp.int32, (64, 128), 1)
    order = jnp.where(d_i == Q * (n_i % 16) + n_i // 16, 1.0, 0.0).astype(BF16)

    send(ro.at[half], ro.at[mate], ro_ss.at[0], ro_rs.at[0], 0, mate).wait_recv()
    for delta in (-1, 1):
        @pl.when(there(delta))
        def _(delta=delta):
            slot = (1 + delta) // 2
            send(
                cot.at[pl.ds(16, 16)], cot.at[pl.ds(16 + 16 * delta, 16)],
                cot_ss.at[slot], cot_rs.at[slot], delta, half,
            ).wait_recv()
    readout = jnp.concatenate([ro[0, 0:1], ro[1, 0:1]], axis=1)
    parts = split3(readout)
    row_i = lax.broadcasted_iota(jnp.int32, (16, 256), 0)
    ro_rows = sum(
        jnp.where(row_i == m, jnp.broadcast_to(part.astype(F32), (16, 256)), 0.0) for m, part in enumerate(parts)
    ).astype(BF16)
    cot_win = cot[pl.ds(pl.multiple_of(8 * half + 8, 8), 24), :]
    cot_t = sum(nt(order, part) for part in split3(cot_win))

    def top(begin, n):
        return jnp.stack(
            [(cot_t[:, i - 8 : i - 7] * readout).reshape(Q, 16, 256) for i in range(begin, begin + n)]
        )

    contacts = {}

    def last_sink(begin, n, x, slope):
        for i in range(max(begin, 16), min(begin + n, 24)):
            flat = x[i - begin].astype(BF16).reshape(64, 256)
            contacts[i] = jnp.sum(nt(ro_rows, flat), axis=0, keepdims=True)
        grad = top(begin, n)
        put(d2, begin - 9, grad * slope, 4)
        low, high = max(begin, 13), min(begin + n, 27)
        if low < high:
            g2[pl.ds(low - 13, high - low)] = grad[low - begin : high - begin]

    forward(2, p2, 5, 9, 22, 11, last_sink)
    clear(d2, 9, 22)
    contact_rows = jnp.concatenate([contacts[i] for i in range(16, 24)], axis=0)
    contact = sum(jnp.dot(part, order, preferred_element_type=F32) for part in split3(contact_rows))

    def backward(k, src, src_first, first, count, before):
        r = 2**k
        lhs = jnp.concatenate(
            [
                src[pl.ds(first - (a - 1) * r - src_first, count), (2 - b) * r : (2 - b) * r + Q].reshape(count * 64, 256)
                for a in range(3) for b in range(3)
            ],
            axis=1,
        )
        wide = jnp.concatenate([w[c, k, a, b] for a in range(3) for b in range(3) for c in range(2)], axis=1)
        return before + nt(lhs, wide).reshape(count, Q, 16, 256)

    grad = backward(2, d2, 9, 13, 14, g2[...])
    put(d1, 0, grad * s1[...], 2)
    clear(d1, 13, 14)
    g1[...] = grad[2:12]
    grad = backward(1, d1, 13, 15, 10, g1[...])
    put(d0, 0, grad * s0[...], 1)
    clear(d0, 15, 10)
    grad = backward(0, d0, 15, 16, 8, grad[1:9])

    spread[...] = jnp.zeros(spread.shape, F32)
    for t in range(8 + Q - 1):
        total = sum(grad[t - q, q] for q in range(Q) if 0 <= t - q < 8)
        place = pl.ds(8 + t, 16, stride=Q)
        for c in range(2):
            spread[c, place, :] = spread[c, place, :] + total[:, 128 * c : 128 * c + 128]

    def rg_source(k, chan):
        return spread.at[chan, pl.ds(pl.multiple_of(8 - 8 * half + 16 * k, 8), 16)]

    def rg_copy(k, chan):
        return send(rg_source(k, chan), rg.at[k, half], rg_ss.at[k, chan], rg_rs.at[k, half], k, chan)

    def each_rg(act):
        for k in (4, 3, 2, 1, 0):
            if k == 0:
                act(rg_copy(0, mate))
            else:
                @pl.when(there(k))
                def _(k=k):
                    for chan in range(2):
                        act(rg_copy(k, chan))

    each_rg(lambda c: c.start())
    lg = jnp.sum(grad.reshape(8, 64, 256), axis=1)
    low, high = lg[:, :128], lg[:, 128:]
    swap_out[0:8] = jnp.where(half == 0, high, low)
    swap_out[8:16] = contact
    swap_copy = send(swap_out, swap, swap_ss.at[0], swap_rs.at[0], 0, mate)
    swap_copy.start()
    rg[0, half] = spread[half, pl.ds(pl.multiple_of(8 - 8 * half, 8), 16), :]
    mine = pl.ds(pl.multiple_of(8 * half, 8), 8)
    other = pl.ds(pl.multiple_of(8 * mate, 8), 8)
    lg_out[mine, :] = jnp.where(half == 0, low, high)
    contact_out[mine, :] = contact[:, :64]

    for k in range(1, 5):
        @pl.when(jnp.logical_not(there(-k)))
        def _(k=k):
            rg[k] = jnp.zeros(rg.shape[1:], F32)

    swap_copy.wait_recv()
    lg_out[other, :] = swap[0:8]
    contact_out[other, :] = swap[8:16, :64]

    def rg_wait(k, chan):
        send(rg_source(k, chan), rg.at[k, chan], rg_ss.at[k, chan], rg_rs.at[k, chan], 0, mate).wait_recv()

    for k in range(5):
        if k == 0:
            rg_wait(0, mate)
        else:
            @pl.when(there(-k))
            def _(k=k):
                for chan in range(2):
                    rg_wait(k, chan)
    rg_out[...] = sum(rg[k, c] for k in range(5) for c in range(2))

    each_emb(lambda c: c.wait_send())
    for k in range(layers):
        w_copy(k).wait_send()
    ro_copy.wait_send()
    each_cot(lambda c: c.wait_send())
    each_rg(lambda c: c.wait_send())
    swap_copy.wait_send()


def local(slabs, left_embed, right_embed, conv_weight, readout, cotangent):
    vmem = pl.BlockSpec(memory_space=pltpu.VMEM)
    dma = pltpu.SemaphoreType.DMA

    def padded(rows, r):
        return pltpu.VMEM((rows, Q + 2 * r, 16, 256), BF16)

    def wide(rows):
        return pltpu.VMEM((rows, Q, 16, 256), F32)

    return pl.pallas_call(
        functools.partial(kernel, slabs),
        out_shape=(
            jax.ShapeDtypeStruct((16, 64), F32),
            jax.ShapeDtypeStruct((16, 128), F32),
            jax.ShapeDtypeStruct((16, 128), F32),
        ),
        in_specs=[vmem, vmem, pl.BlockSpec(memory_space=pl.ANY), vmem, vmem],
        out_specs=(vmem, vmem, vmem),
        scratch_shapes=[
            pltpu.VMEM((32, 128), BF16),
            pltpu.VMEM((7, 2, 32, 128), BF16),
            pltpu.VMEM((4, 112, 128), F32),
            pltpu.VMEM((2, 3, 3, 3, 256, 128), BF16),
            pltpu.VMEM((48, 128), F32),
            pltpu.VMEM((2, 8, 128), F32),
            padded(36, 1), padded(34, 2), padded(30, 4),
            padded(22, 4), padded(14, 2), padded(10, 1),
            wide(10), wide(14), wide(14), wide(10),
            pltpu.VMEM((2, 88, 128), F32),
            pltpu.VMEM((5, 2, 16, 128), F32),
            pltpu.VMEM((16, 128), F32),
            pltpu.VMEM((16, 128), F32),
            dma((7, 2)), dma((7, 2)), dma((3,)), dma((3,)), dma((3,)),
            dma((2,)), dma((2,)), dma((1,)), dma((1,)),
            dma((5, 2)), dma((5, 2)), dma((1,)), dma((1,)),
        ],
        compiler_params=pltpu.CompilerParams(
            collective_id=0, has_side_effects=True, vmem_limit_bytes=56 * 2**20
        ),
        cost_estimate=pl.CostEstimate(flops=8 * 10**9, bytes_accessed=4 * 10**6, transcendentals=10**6),
    )(left_embed, right_embed, conv_weight, readout.reshape(1, 128), cotangent)


def solution(mesh):
    return jax.shard_map(
        functools.partial(local, mesh.shape["chrom"]),
        mesh=mesh,
        in_specs=(
            P("chrom", "chan"),
            P("chrom", "chan"),
            P(None, None, None, None, "chan"),
            P("chan"),
            P("chrom", None),
        ),
        out_specs=(P("chrom", None), P("chrom", "chan"), P("chrom", "chan")),
        check_vma=False,
    )
```

time: 211 us -> 36.4 us (0.17)
  the two profiles are of different devices: /device:TPU:8 before, /device:TPU:9 now
where the time goes in v1:
time: 36.4 us; the launch traced here: 36 us
  Pallas kernels  31.5 us (87%)
  local copies, waits for them, and re-layouts  3.89 us (11%)
  between operations  0.64 us (2%)
    pallas_call x1, Pallas kernels, local(): pl.pallas_call(functools.partial(kernel, slabs), out_shape=(jax.ShapeDtyp...  31.5 us
    unnamed x3, local copies, waits for them, and re-layouts  3.89 us

profile of v1, /device:TPU:9, one launch (start us, length us, event | category | flops | bytes accessed | tf_op | source)
XLA Modules:
  0.0 36.0 jit_solution(6378176331635877606)
XLA Ops:
  0.6 31.5 %shard_map.76 = (f32[16,64]{1,0:T(8,128)}, f32[16,128]{1,0:T(8,128)}, f32[16,128]{1,0:T(8,128)}) custom-call(bf16[16,128]{1,0:T(8,128)(2,1)} %left_ref.1, bf16[16,128]{1,0:T(8,128)(2,1)} %right_ref.1, bf16[3,3,3,256,128]{4,3,2,1,0:T(8,128)(2,1)} %w_hbm.1, f32[1,128]{1,0:T(1,128)} %bitcast.1, f32[16,64]{1,0:T(8,128)} %cot_ref.1), custom_call_target="tpu_custom_call" | custom-call | flops 8000000000 | bytes 4000000 | tf_op jit(solution)/shard_map/pallas_call | solution.py:363
  32.1 1.3 %copy.11 = f32[16,64]{1,0:T(8,128)} copy(f32[16,64]{1,0:T(8,128)} %get-tuple-element.6) | data formatting | bytes 8192
  33.4 1.3 %copy.12 = f32[16,128]{1,0:T(8,128)} copy(f32[16,128]{1,0:T(8,128)} %get-tuple-element.7) | data formatting | bytes 16384
  34.7 1.3 %copy.13 = f32[16,128]{1,0:T(8,128)} copy(f32[16,128]{1,0:T(8,128)} %get-tuple-element.8) | data formatting | bytes 16384

commit v2 on v1

--- a/solution.py
+++ b/solution.py
@@ -44,9 +44,9 @@
     slabs,
     left_ref, right_ref, w_hbm, ro_ref, cot_ref,
     contact_out, lg_out, rg_out,
-    block, emb, rwin, w, cot, ro, p0, p1, p2, d2, d1, d0, s0, s1, g2, g1,
+    block, emb, rwin, w, cot, ro, p0, p1, p2, d2, d1, d0, s0, s1, g2, g1, g0,
     spread, rg, swap_out, swap,
-    emb_ss, emb_rs, w_ls, w_ss, w_rs, cot_ss, cot_rs, ro_ss, ro_rs, rg_ss, rg_rs, swap_ss, swap_rs,
+    emb_ss, emb_rs, w_ls, w_ss, w_rs, cot_ss, cot_rs, ro_ss, ro_rs, rg_ss, rg_rs, swap_ss, swap_rs, rim_ss, rim_rs,
 ):
     slab = lax.axis_index("chrom")
     half = lax.axis_index("chan")
@@ -148,75 +148,91 @@
             rwin[c, 16 * k : 16 * k + 16] = emb[k, c, 0:16].astype(F32)
             if k < 3:
                 rwin[2 + c, 16 * k : 16 * k + 16] = emb[k, c, 16:32].astype(F32)
-    start = pl.multiple_of(8 * half, 8)
-    for c in range(2):
-        rwin[c, 0:104] = rwin[c, pl.ds(start, 104)]
-    lwin = jnp.concatenate([rwin[2 + c, pl.ds(start, 40)] for c in range(2)], axis=1)
-
-    def clear(buf, first, count):
-        for h in range(2):
-            low, high = 16 - 8 * h, 32 - 8 * h
-            if first < low:
-                @pl.when(jnp.logical_and(slab == 0, half == h))
-                def _():
-                    n = min(low, first + count) - first
-                    buf[0:n] = jnp.zeros((n,) + buf.shape[1:], BF16)
-            if first + count > high:
-                @pl.when(jnp.logical_and(slab == slabs - 1, half == h))
-                def _():
-                    begin = max(high - first, 0)
-                    buf[begin:count] = jnp.zeros((count - begin,) + buf.shape[1:], BF16)
-
-    diag = {}
-    for i in range(36):
-        tiles = []
-        for q in range(Q):
-            t = 2 + i + q
-            if t not in diag:
-                diag[t] = jnp.concatenate([rwin[c, pl.ds(t, 16, stride=Q), :] for c in range(2)], axis=1)
-            tiles.append(diag[t] + lwin[2 + i : 3 + i, :])
-        put(p0, i, jnp.stack(tiles)[None], 1)
-    clear(p0, 2, 36)
+
+    sign = 2 * half - 1
+
+    def bin_of(v):
+        return 7 + half + sign * v
+
+    outer_edge = jnp.logical_or(
+        jnp.logical_and(half == 0, slab == 0), jnp.logical_and(half == 1, slab == slabs - 1)
+    )
+
+    def clear(buf, r):
+        @pl.when(outer_edge)
+        def _():
+            buf[r + 8 :] = jnp.zeros((buf.shape[0] - r - 8,) + buf.shape[1:], BF16)
+
+    def rim(n, buf, r):
+        return [
+            send(buf.at[r + j], buf.at[r - 1 - j], rim_ss.at[n, j], rim_rs.at[n, j], 0, mate)
+            for j in range(r)
+        ]
+
+    rims = [rim(n, buf, r) for n, (buf, r) in enumerate([(p1, 2), (p2, 4), (d2, 4), (d1, 2), (d0, 1)])]
+
+    def rim_start(n):
+        for copy in rims[n]:
+            copy.start()
+
+    def rim_wait(n):
+        for copy in rims[n]:
+            copy.wait_recv()
+
+    for v in range(-1, 22):
+        place = 16 + bin_of(v)
+        left = jnp.concatenate([rwin[2 + c, pl.ds(place, 1), :] for c in range(2)], axis=1)
+        tiles = [
+            left + jnp.concatenate([rwin[c, pl.ds(place + q, 16, stride=Q), :] for c in range(2)], axis=1)
+            for q in range(Q)
+        ]
+        put(p0, v + 1, jnp.stack(tiles)[None], 1)
+    clear(p0, 1)
+
+    taps = [2 - 2 * half, 1, 2 * half]
 
     def weights(k):
         local[k].wait()
         send(w_hbm.at[k], w.at[mate, k], w_ss.at[k], w_rs.at[k], 0, mate).wait_recv()
 
-    def forward(k, src, src_first, first, count, chunk, sink):
+    def forward(k, src, chunks, sink):
         r = 2**k
         weights(k)
-        wide = jnp.concatenate([w[c, k].reshape(9 * 256, 128) for c in range(2)], axis=1)
-        for begin in range(first, first + count, chunk):
-            n = min(chunk, first + count - begin)
+        wide = jnp.concatenate(
+            [jnp.concatenate([w[c, k, a].reshape(3 * 256, 128) for a in taps], axis=0) for c in range(2)], axis=1
+        )
+        begin = 0
+        for n in chunks:
             lhs = jnp.concatenate(
                 [
-                    src[pl.ds(begin + (a - 1) * r - src_first, n), b * r : b * r + Q].reshape(n * 64, 256)
-                    for a in range(3) for b in range(3)
+                    src[pl.ds(begin + m * r, n), b * r : b * r + Q].reshape(n * 64, 256)
+                    for m in range(3) for b in range(3)
                 ],
                 axis=1,
             )
             z = jnp.dot(lhs, wide, preferred_element_type=F32).reshape(n, Q, 16, 256)
             s = 0.5 + 0.5 * jnp.tanh(0.5 * z)
-            old = src[pl.ds(begin - src_first, n), r : r + Q].astype(F32)
+            old = src[pl.ds(begin + r, n), r : r + Q].astype(F32)
             zs = z * s
             sink(begin, n, old + zs, s + zs * (1.0 - s))
-
-    def keep(buf, buf_first, r, slopes, slopes_first):
-        count = slopes.shape[0]
-
+            begin += n
+
+    def keep(buf, r, slopes, n_rim):
         def sink(begin, n, x, slope):
-            if buf is not None:
-                put(buf, begin - buf_first, x, r)
-            low, high = max(begin, slopes_first), min(begin + n, slopes_first + count)
-            if low < high:
-                slopes[pl.ds(low - slopes_first, high - low)] = slope[low - begin : high - begin]
+            put(buf, begin + r, x, r)
+            if begin == 0:
+                rim_start(n_rim)
+            kept = min(begin + n, slopes.shape[0]) - begin
+            if kept > 0:
+                slopes[pl.ds(begin, kept)] = slope[:kept]
 
         return sink
 
-    forward(0, p0, 2, 3, 34, 9, keep(p1, 3, 2, s0, 15))
-    clear(p1, 3, 34)
-    forward(1, p1, 3, 5, 30, 10, keep(p2, 5, 4, s1, 13))
-    clear(p2, 5, 30)
+    forward(0, p0, (11, 10), keep(p1, 2, s0, 0))
+    clear(p1, 2)
+    rim_wait(0)
+    forward(1, p1, (10, 9), keep(p2, 4, s1, 1))
+    clear(p2, 4)
 
     n_i = lax.broadcasted_iota(jnp.int32, (64, 128), 0)
     d_i = lax.broadcasted_iota(jnp.int32, (64, 128), 1)
@@ -237,55 +253,77 @@
     ro_rows = sum(
         jnp.where(row_i == m, jnp.broadcast_to(part.astype(F32), (16, 256)), 0.0) for m, part in enumerate(parts)
     ).astype(BF16)
-    cot_win = cot[pl.ds(pl.multiple_of(8 * half + 8, 8), 24), :]
+    cot_win = jnp.concatenate([cot[pl.ds(16 + bin_of(v), 1), :] for v in range(16)], axis=0)
     cot_t = sum(nt(order, part) for part in split3(cot_win))
 
-    def top(begin, n):
-        return jnp.stack(
-            [(cot_t[:, i - 8 : i - 7] * readout).reshape(Q, 16, 256) for i in range(begin, begin + n)]
+    contacts = {}
+
+    def last_sink(begin, n, x, slope):
+        grad = jnp.stack(
+            [(cot_t[:, v : v + 1] * readout).reshape(Q, 16, 256) for v in range(begin, begin + n)]
         )
-
-    contacts = {}
-
-    def last_sink(begin, n, x, slope):
-        for i in range(max(begin, 16), min(begin + n, 24)):
-            flat = x[i - begin].astype(BF16).reshape(64, 256)
-            contacts[i] = jnp.sum(nt(ro_rows, flat), axis=0, keepdims=True)
-        grad = top(begin, n)
-        put(d2, begin - 9, grad * slope, 4)
-        low, high = max(begin, 13), min(begin + n, 27)
-        if low < high:
-            g2[pl.ds(low - 13, high - low)] = grad[low - begin : high - begin]
-
-    forward(2, p2, 5, 9, 22, 11, last_sink)
-    clear(d2, 9, 22)
-    contact_rows = jnp.concatenate([contacts[i] for i in range(16, 24)], axis=0)
+        put(d2, begin + 4, grad * slope, 4)
+        if begin == 0:
+            rim_start(2)
+        kept = min(begin + n, 11) - begin
+        if kept > 0:
+            g2[pl.ds(begin, kept)] = grad[:kept]
+        for v in range(begin, min(begin + n, 8)):
+            flat = x[v - begin].astype(BF16).reshape(64, 256)
+            contacts[v] = jnp.sum(nt(ro_rows, flat), axis=0, keepdims=True)
+
+    rim_wait(1)
+    forward(2, p2, (8, 7), last_sink)
+    clear(d2, 4)
+    outwards = jnp.concatenate([contacts[v] for v in range(8)], axis=0)
+    inwards = jnp.concatenate([contacts[7 - v] for v in range(8)], axis=0)
+    contact_rows = jnp.where(half == 1, outwards, inwards)
     contact = sum(jnp.dot(part, order, preferred_element_type=F32) for part in split3(contact_rows))
 
-    def backward(k, src, src_first, first, count, before):
+    def backward(k, src, chunks, before, sink):
         r = 2**k
-        lhs = jnp.concatenate(
-            [
-                src[pl.ds(first - (a - 1) * r - src_first, count), (2 - b) * r : (2 - b) * r + Q].reshape(count * 64, 256)
-                for a in range(3) for b in range(3)
-            ],
-            axis=1,
-        )
-        wide = jnp.concatenate([w[c, k, a, b] for a in range(3) for b in range(3) for c in range(2)], axis=1)
-        return before + nt(lhs, wide).reshape(count, Q, 16, 256)
-
-    grad = backward(2, d2, 9, 13, 14, g2[...])
-    put(d1, 0, grad * s1[...], 2)
-    clear(d1, 13, 14)
-    g1[...] = grad[2:12]
-    grad = backward(1, d1, 13, 15, 10, g1[...])
-    put(d0, 0, grad * s0[...], 1)
-    clear(d0, 15, 10)
-    grad = backward(0, d0, 15, 16, 8, grad[1:9])
+        wide = jnp.concatenate([w[c, k, a, b] for a in taps for b in range(3) for c in range(2)], axis=1)
+        begin = 0
+        for n in chunks:
+            lhs = jnp.concatenate(
+                [
+                    src[pl.ds(begin + (2 - m) * r, n), (2 - b) * r : (2 - b) * r + Q].reshape(n * 64, 256)
+                    for m in range(3) for b in range(3)
+                ],
+                axis=1,
+            )
+            sink(begin, n, before[pl.ds(begin, n)] + nt(lhs, wide).reshape(n, Q, 16, 256))
+            begin += n
+
+    def hand_on(buf, r, slopes, grads, n_rim):
+        def sink(begin, n, grad):
+            put(buf, begin + r, grad * slopes[pl.ds(begin, n)], r)
+            if begin == 0:
+                rim_start(n_rim)
+            kept = min(begin + n, grads.shape[0]) - begin
+            if kept > 0:
+                grads[pl.ds(begin, kept)] = grad[:kept]
+
+        return sink
+
+    def last(begin, n, grad):
+        g0[pl.ds(begin, n)] = grad
+
+    rim_wait(2)
+    backward(2, d2, (6, 5), g2, hand_on(d1, 2, s1, g1, 3))
+    clear(d1, 2)
+    rim_wait(3)
+    backward(1, d1, (5, 4), g1, hand_on(d0, 1, s0, g0, 4))
+    clear(d0, 1)
+    rim_wait(4)
+    backward(0, d0, (8,), g0, last)
+
+    def v_of(u):
+        return (1 - half) * (7 - u) + half * u
 
     spread[...] = jnp.zeros(spread.shape, F32)
     for t in range(8 + Q - 1):
-        total = sum(grad[t - q, q] for q in range(Q) if 0 <= t - q < 8)
+        total = sum(g0[v_of(t - q), q] for q in range(Q) if 0 <= t - q < 8)
         place = pl.ds(8 + t, 16, stride=Q)
         for c in range(2):
             spread[c, place, :] = spread[c, place, :] + total[:, 128 * c : 128 * c + 128]
@@ -307,7 +345,9 @@
                         act(rg_copy(k, chan))
 
     each_rg(lambda c: c.start())
-    lg = jnp.sum(grad.reshape(8, 64, 256), axis=1)
+    lg = jnp.concatenate(
+        [jnp.sum(g0[v_of(u)].reshape(64, 256), axis=0, keepdims=True) for u in range(8)], axis=0
+    )
     low, high = lg[:, :128], lg[:, 128:]
     swap_out[0:8] = jnp.where(half == 0, high, low)
     swap_out[8:16] = contact
@@ -348,10 +388,23 @@
     each_cot(lambda c: c.wait_send())
     each_rg(lambda c: c.wait_send())
     swap_copy.wait_send()
+    for copies in rims:
+        for copy in copies:
+            copy.wait_send()
+
+
+def hand_out(*refs):
+    sems = refs[6]
+    copies = [pltpu.make_async_copy(refs[n], refs[3 + n], sems.at[n]) for n in range(3)]
+    for copy in copies:
+        copy.start()
+    for copy in copies:
+        copy.wait()
 
 
 def local(slabs, left_embed, right_embed, conv_weight, readout, cotangent):
     vmem = pl.BlockSpec(memory_space=pltpu.VMEM)
+    anywhere = pl.BlockSpec(memory_space=pl.ANY)
     dma = pltpu.SemaphoreType.DMA
 
     def padded(rows, r):
@@ -360,14 +413,15 @@
     def wide(rows):
         return pltpu.VMEM((rows, Q, 16, 256), F32)
 
-    return pl.pallas_call(
+    out_shape = (
+        jax.ShapeDtypeStruct((16, 64), F32),
+        jax.ShapeDtypeStruct((16, 128), F32),
+        jax.ShapeDtypeStruct((16, 128), F32),
+    )
+    results = pl.pallas_call(
         functools.partial(kernel, slabs),
-        out_shape=(
-            jax.ShapeDtypeStruct((16, 64), F32),
-            jax.ShapeDtypeStruct((16, 128), F32),
-            jax.ShapeDtypeStruct((16, 128), F32),
-        ),
-        in_specs=[vmem, vmem, pl.BlockSpec(memory_space=pl.ANY), vmem, vmem],
+        out_shape=out_shape,
+        in_specs=[vmem, vmem, anywhere, vmem, vmem],
         out_specs=(vmem, vmem, vmem),
         scratch_shapes=[
             pltpu.VMEM((32, 128), BF16),
@@ -376,9 +430,9 @@
             pltpu.VMEM((2, 3, 3, 3, 256, 128), BF16),
             pltpu.VMEM((48, 128), F32),
             pltpu.VMEM((2, 8, 128), F32),
-            padded(36, 1), padded(34, 2), padded(30, 4),
-            padded(22, 4), padded(14, 2), padded(10, 1),
-            wide(10), wide(14), wide(14), wide(10),
+            padded(23, 1), padded(23, 2), padded(23, 4),
+            padded(19, 4), padded(13, 2), padded(10, 1),
+            wide(9), wide(11), wide(11), wide(9), wide(8),
             pltpu.VMEM((2, 88, 128), F32),
             pltpu.VMEM((5, 2, 16, 128), F32),
             pltpu.VMEM((16, 128), F32),
@@ -386,12 +440,17 @@
             dma((7, 2)), dma((7, 2)), dma((3,)), dma((3,)), dma((3,)),
             dma((2,)), dma((2,)), dma((1,)), dma((1,)),
             dma((5, 2)), dma((5, 2)), dma((1,)), dma((1,)),
+            dma((5, 4)), dma((5, 4)),
         ],
         compiler_params=pltpu.CompilerParams(
             collective_id=0, has_side_effects=True, vmem_limit_bytes=56 * 2**20
         ),
         cost_estimate=pl.CostEstimate(flops=8 * 10**9, bytes_accessed=4 * 10**6, transcendentals=10**6),
     )(left_embed, right_embed, conv_weight, readout.reshape(1, 128), cotangent)
+    return pl.pallas_call(
+        hand_out, out_shape=out_shape, in_specs=[anywhere] * 3, out_specs=(anywhere,) * 3,
+        scratch_shapes=[dma((3,))],
+    )(*results)
 
 
 def solution(mesh):

time: 36.4 us -> 33.5 us (0.920)
  local copies, waits for them, and re-layouts: 3.89 us -> 0 us
  Pallas kernels: 31.5 us -> 32.7 us
    unnamed x3 -> x0, local copies, waits for them, and re-layouts: 3.89 us -> none
    pallas_call x1 -> x2, Pallas kernels: 31.5 us -> 32.7 us  [the longest x1 30.8 us: local(): pl.pallas_call(functools.partial(kernel, slabs), out_shape=out_shape, in_...]
where the time goes in v2:
time: 33.5 us; the launch traced here: 33.3 us
  Pallas kernels  32.7 us (98%)
  between operations  0.64 us (2%)
    pallas_call x1, Pallas kernels, local(): pl.pallas_call(functools.partial(kernel, slabs), out_shape=out_shape, in_...  30.8 us
    pallas_call x1, Pallas kernels, local(): pl.pallas_call(hand_out, out_shape=out_shape, in_specs=[anywhere] * 3, ou...  1.88 us

profile of v2, /device:TPU:9, one launch (start us, length us, event | category | flops | bytes accessed | tf_op | source)
XLA Modules:
  0.0 33.3 jit_solution(4498345989079794886)
XLA Ops:
  0.6 30.8 %shard_map.76 = (f32[16,64]{1,0:T(8,128)}, f32[16,128]{1,0:T(8,128)}, f32[16,128]{1,0:T(8,128)}) custom-call(bf16[16,128]{1,0:T(8,128)(2,1)} %left_ref.1, bf16[16,128]{1,0:T(8,128)(2,1)} %right_ref.1, bf16[3,3,3,256,128]{4,3,2,1,0:T(8,128)(2,1)} %w_hbm.1, f32[1,128]{1,0:T(1,128)} %bitcast.1, f32[16,64]{1,0:T(8,128)} %cot_ref.1), custom_call_target="tpu_custom_call" | custom-call | flops 8000000000 | bytes 4000000 | tf_op jit(solution)/shard_map/pallas_call | solution.py:421
  31.4 1.9 %shard_map.77 = (f32[16,64]{1,0:T(8,128)}, f32[16,128]{1,0:T(8,128)}, f32[16,128]{1,0:T(8,128)}) custom-call(f32[16,64]{1,0:T(8,128)} %get-tuple-element.6.refs_0_, f32[16,128]{1,0:T(8,128)} %get-tuple-element.7.refs_1_, f32[16,128]{1,0:T(8,128)} %get-tuple-element.8.refs_2_), custom_call_target="tpu_custom_call" | custom-call | tf_op jit(solution)/shard_map/pallas_call | solution.py:450

commit v3 on v2

--- a/solution.py
+++ b/solution.py
@@ -44,7 +44,7 @@
     slabs,
     left_ref, right_ref, w_hbm, ro_ref, cot_ref,
     contact_out, lg_out, rg_out,
-    block, emb, rwin, w, cot, ro, p0, p1, p2, d2, d1, d0, s0, s1, g2, g1, g0,
+    block, emb, rwin, w, cot, ro, p0, p1, p2, d2, d1, d0, s0, s1, g2, g1, g0, columns, p3,
     spread, rg, swap_out, swap,
     emb_ss, emb_rs, w_ls, w_ss, w_rs, cot_ss, cot_rs, ro_ss, ro_rs, rg_ss, rg_rs, swap_ss, swap_rs, rim_ss, rim_rs,
 ):
@@ -179,14 +179,17 @@
         for copy in rims[n]:
             copy.wait_recv()
 
-    for v in range(-1, 22):
-        place = 16 + bin_of(v)
+    def first_pair(row, unused):
+        place = 16 + bin_of(row - 1)
         left = jnp.concatenate([rwin[2 + c, pl.ds(place, 1), :] for c in range(2)], axis=1)
         tiles = [
             left + jnp.concatenate([rwin[c, pl.ds(place + q, 16, stride=Q), :] for c in range(2)], axis=1)
             for q in range(Q)
         ]
-        put(p0, v + 1, jnp.stack(tiles)[None], 1)
+        put(p0, row, jnp.stack(tiles)[None], 1)
+        return unused
+
+    lax.fori_loop(0, 23, first_pair, 0)
     clear(p0, 1)
 
     taps = [2 - 2 * half, 1, 2 * half]
@@ -195,14 +198,16 @@
         local[k].wait()
         send(w_hbm.at[k], w.at[mate, k], w_ss.at[k], w_rs.at[k], 0, mate).wait_recv()
 
-    def forward(k, src, chunks, sink):
+    def forward(k, src, steps, n, sink):
         r = 2**k
         weights(k)
-        wide = jnp.concatenate(
-            [jnp.concatenate([w[c, k, a].reshape(3 * 256, 128) for a in taps], axis=0) for c in range(2)], axis=1
-        )
-        begin = 0
-        for n in chunks:
+
+        def step(index, unused):
+            begin = index * n
+            wide = jnp.concatenate(
+                [jnp.concatenate([w[c, k, a].reshape(3 * 256, 128) for a in taps], axis=0) for c in range(2)],
+                axis=1,
+            )
             lhs = jnp.concatenate(
                 [
                     src[pl.ds(begin + m * r, n), b * r : b * r + Q].reshape(n * 64, 256)
@@ -214,24 +219,28 @@
             s = 0.5 + 0.5 * jnp.tanh(0.5 * z)
             old = src[pl.ds(begin + r, n), r : r + Q].astype(F32)
             zs = z * s
-            sink(begin, n, old + zs, s + zs * (1.0 - s))
-            begin += n
+            sink(index, begin, n, old + zs, s + zs * (1.0 - s))
+            return unused
+
+        lax.fori_loop(0, steps, step, 0)
+
+    def rim_after(index, n_rim):
+        @pl.when(index == 0)
+        def _():
+            rim_start(n_rim)
 
     def keep(buf, r, slopes, n_rim):
-        def sink(begin, n, x, slope):
+        def sink(index, begin, n, x, slope):
             put(buf, begin + r, x, r)
-            if begin == 0:
-                rim_start(n_rim)
-            kept = min(begin + n, slopes.shape[0]) - begin
-            if kept > 0:
-                slopes[pl.ds(begin, kept)] = slope[:kept]
+            rim_after(index, n_rim)
+            slopes[pl.ds(begin, n)] = slope
 
         return sink
 
-    forward(0, p0, (11, 10), keep(p1, 2, s0, 0))
+    forward(0, p0, 3, 7, keep(p1, 2, s0, 0))
     clear(p1, 2)
     rim_wait(0)
-    forward(1, p1, (10, 9), keep(p2, 4, s1, 1))
+    forward(1, p1, 4, 5, keep(p2, 4, s1, 1))
     clear(p2, 4)
 
     n_i = lax.broadcasted_iota(jnp.int32, (64, 128), 0)
@@ -256,35 +265,35 @@
     cot_win = jnp.concatenate([cot[pl.ds(16 + bin_of(v), 1), :] for v in range(16)], axis=0)
     cot_t = sum(nt(order, part) for part in split3(cot_win))
 
-    contacts = {}
-
-    def last_sink(begin, n, x, slope):
-        grad = jnp.stack(
-            [(cot_t[:, v : v + 1] * readout).reshape(Q, 16, 256) for v in range(begin, begin + n)]
-        )
+    for v in range(16):
+        columns[v] = jnp.broadcast_to(cot_t[:, v : v + 1], (64, 128))
+
+    def last_sink(index, begin, n, x, slope):
+        column = columns[pl.ds(begin, n)]
+        grad = jnp.concatenate([column, column], axis=2) * readout[None]
+        grad = grad.reshape(n, Q, 16, 256)
         put(d2, begin + 4, grad * slope, 4)
-        if begin == 0:
-            rim_start(2)
-        kept = min(begin + n, 11) - begin
-        if kept > 0:
-            g2[pl.ds(begin, kept)] = grad[:kept]
-        for v in range(begin, min(begin + n, 8)):
-            flat = x[v - begin].astype(BF16).reshape(64, 256)
-            contacts[v] = jnp.sum(nt(ro_rows, flat), axis=0, keepdims=True)
+        rim_after(index, 2)
+        g2[pl.ds(begin, n)] = grad
+        p3[pl.ds(begin, n)] = x.astype(BF16)
 
     rim_wait(1)
-    forward(2, p2, (8, 7), last_sink)
+    forward(2, p2, 3, 5, last_sink)
     clear(d2, 4)
-    outwards = jnp.concatenate([contacts[v] for v in range(8)], axis=0)
-    inwards = jnp.concatenate([contacts[7 - v] for v in range(8)], axis=0)
+    contacts = [
+        jnp.sum(nt(ro_rows, p3[v].reshape(64, 256)), axis=0, keepdims=True) for v in range(8)
+    ]
+    outwards = jnp.concatenate(contacts, axis=0)
+    inwards = jnp.concatenate(contacts[::-1], axis=0)
     contact_rows = jnp.where(half == 1, outwards, inwards)
     contact = sum(jnp.dot(part, order, preferred_element_type=F32) for part in split3(contact_rows))
 
-    def backward(k, src, chunks, before, sink):
+    def backward(k, src, steps, n, before, sink):
         r = 2**k
-        wide = jnp.concatenate([w[c, k, a, b] for a in taps for b in range(3) for c in range(2)], axis=1)
-        begin = 0
-        for n in chunks:
+
+        def step(index, unused):
+            begin = index * n
+            wide = jnp.concatenate([w[c, k, a, b] for a in taps for b in range(3) for c in range(2)], axis=1)
             lhs = jnp.concatenate(
                 [
                     src[pl.ds(begin + (2 - m) * r, n), (2 - b) * r : (2 - b) * r + Q].reshape(n * 64, 256)
@@ -292,31 +301,30 @@
                 ],
                 axis=1,
             )
-            sink(begin, n, before[pl.ds(begin, n)] + nt(lhs, wide).reshape(n, Q, 16, 256))
-            begin += n
+            sink(index, begin, n, before[pl.ds(begin, n)] + nt(lhs, wide).reshape(n, Q, 16, 256))
+            return unused
+
+        lax.fori_loop(0, steps, step, 0)
 
     def hand_on(buf, r, slopes, grads, n_rim):
-        def sink(begin, n, grad):
+        def sink(index, begin, n, grad):
             put(buf, begin + r, grad * slopes[pl.ds(begin, n)], r)
-            if begin == 0:
-                rim_start(n_rim)
-            kept = min(begin + n, grads.shape[0]) - begin
-            if kept > 0:
-                grads[pl.ds(begin, kept)] = grad[:kept]
+            rim_after(index, n_rim)
+            grads[pl.ds(begin, n)] = grad
 
         return sink
 
-    def last(begin, n, grad):
+    def last(index, begin, n, grad):
         g0[pl.ds(begin, n)] = grad
 
     rim_wait(2)
-    backward(2, d2, (6, 5), g2, hand_on(d1, 2, s1, g1, 3))
+    backward(2, d2, 2, 6, g2, hand_on(d1, 2, s1, g1, 3))
     clear(d1, 2)
     rim_wait(3)
-    backward(1, d1, (5, 4), g1, hand_on(d0, 1, s0, g0, 4))
+    backward(1, d1, 2, 5, g1, hand_on(d0, 1, s0, g0, 4))
     clear(d0, 1)
     rim_wait(4)
-    backward(0, d0, (8,), g0, last)
+    backward(0, d0, 2, 4, g0, last)
 
     def v_of(u):
         return (1 - half) * (7 - u) + half * u
@@ -430,9 +438,10 @@
             pltpu.VMEM((2, 3, 3, 3, 256, 128), BF16),
             pltpu.VMEM((48, 128), F32),
             pltpu.VMEM((2, 8, 128), F32),
-            padded(23, 1), padded(23, 2), padded(23, 4),
-            padded(19, 4), padded(13, 2), padded(10, 1),
-            wide(9), wide(11), wide(11), wide(9), wide(8),
+            padded(23, 1), padded(24, 2), padded(24, 4),
+            padded(20, 4), padded(14, 2), padded(11, 1),
+            wide(21), wide(20), wide(15), wide(12), wide(10),
+            pltpu.VMEM((16, 64, 128), F32), pltpu.VMEM((15, Q, 16, 256), BF16),
             pltpu.VMEM((2, 88, 128), F32),
             pltpu.VMEM((5, 2, 16, 128), F32),
             pltpu.VMEM((16, 128), F32),

time: 33.5 us -> 31 us (0.925)
  Pallas kernels: 32.7 us -> 30.1 us
    pallas_call x1, Pallas kernels: 30.8 us -> 28.2 us  [local(): pl.pallas_call(functools.partial(kernel, slabs), out_shape=out_shape, in_...]
where the time goes in v3:
time: 31 us; the launch traced here: 30.7 us
  Pallas kernels  30.1 us (97%)
  between operations  0.64 us (2%)
    pallas_call x1, Pallas kernels, local(): pl.pallas_call(functools.partial(kernel, slabs), out_shape=out_shape, in_...  28.2 us
    pallas_call x1, Pallas kernels, local(): pl.pallas_call(hand_out, out_shape=out_shape, in_specs=[anywhere] * 3, ou...  1.88 us

profile of v3, /device:TPU:9, one launch (start us, length us, event | category | flops | bytes accessed | tf_op | source)
XLA Modules:
  0.0 30.7 jit_solution(12432901113230597462)
XLA Ops:
  0.6 28.2 %shard_map.76 = (f32[16,64]{1,0:T(8,128)}, f32[16,128]{1,0:T(8,128)}, f32[16,128]{1,0:T(8,128)}) custom-call(bf16[16,128]{1,0:T(8,128)(2,1)} %left_ref.1, bf16[16,128]{1,0:T(8,128)(2,1)} %right_ref.1, bf16[3,3,3,256,128]{4,3,2,1,0:T(8,128)(2,1)} %w_hbm.1, f32[1,128]{1,0:T(1,128)} %bitcast.1, f32[16,64]{1,0:T(8,128)} %cot_ref.1), custom_call_target="tpu_custom_call" | custom-call | flops 8000000000 | bytes 4000000 | tf_op jit(solution)/shard_map/pallas_call | solution.py:429
  28.9 1.9 %shard_map.77 = (f32[16,64]{1,0:T(8,128)}, f32[16,128]{1,0:T(8,128)}, f32[16,128]{1,0:T(8,128)}) custom-call(f32[16,64]{1,0:T(8,128)} %get-tuple-element.6.refs_0_, f32[16,128]{1,0:T(8,128)} %get-tuple-element.7.refs_1_, f32[16,128]{1,0:T(8,128)} %get-tuple-element.8.refs_2_), custom_call_target="tpu_custom_call" | custom-call | tf_op jit(solution)/shard_map/pallas_call | solution.py:459

commit v4 on v3

--- a/solution.py
+++ b/solution.py
@@ -109,8 +109,10 @@
                     for chan in range(2):
                         act(emb_copy(delta, chan))
 
-    def w_copy(k):
-        return send(w_hbm.at[k], w.at[half, k], w_ss.at[k], w_rs.at[k], 0, mate)
+    def w_copy(k, a):
+        return send(w_hbm.at[k, a], w.at[half, k, a], w_ss.at[k, a], w_rs.at[k, a], 0, mate)
+
+    every_w = [(k, a) for k in range(layers) for a in range(3)]
 
     def cot_copy(delta):
         place = pl.ds(16 - 16 * delta, 16)
@@ -126,8 +128,8 @@
     ro_copy = send(ro.at[half], ro.at[half], ro_ss.at[0], ro_rs.at[0], 0, mate)
 
     each_emb(lambda c: c.start())
-    for k in range(layers):
-        w_copy(k).start()
+    for k, a in every_w:
+        w_copy(k, a).start()
     ro_copy.start()
     each_cot(lambda c: c.start())
 
@@ -189,14 +191,15 @@
         put(p0, row, jnp.stack(tiles)[None], 1)
         return unused
 
-    lax.fori_loop(0, 23, first_pair, 0)
+    lax.fori_loop(0, 24, first_pair, 0)
     clear(p0, 1)
 
     taps = [2 - 2 * half, 1, 2 * half]
 
     def weights(k):
         local[k].wait()
-        send(w_hbm.at[k], w.at[mate, k], w_ss.at[k], w_rs.at[k], 0, mate).wait_recv()
+        for a in range(3):
+            send(w_hbm.at[k, a], w.at[mate, k, a], w_ss.at[k, a], w_rs.at[k, a], 0, mate).wait_recv()
 
     def forward(k, src, steps, n, sink):
         r = 2**k
@@ -237,10 +240,10 @@
 
         return sink
 
-    forward(0, p0, 3, 7, keep(p1, 2, s0, 0))
+    forward(0, p0, 2, 11, keep(p1, 2, s0, 0))
     clear(p1, 2)
     rim_wait(0)
-    forward(1, p1, 4, 5, keep(p2, 4, s1, 1))
+    forward(1, p1, 2, 10, keep(p2, 4, s1, 1))
     clear(p2, 4)
 
     n_i = lax.broadcasted_iota(jnp.int32, (64, 128), 0)
@@ -278,7 +281,7 @@
         p3[pl.ds(begin, n)] = x.astype(BF16)
 
     rim_wait(1)
-    forward(2, p2, 3, 5, last_sink)
+    forward(2, p2, 2, 8, last_sink)
     clear(d2, 4)
     contacts = [
         jnp.sum(nt(ro_rows, p3[v].reshape(64, 256)), axis=0, keepdims=True) for v in range(8)
@@ -324,7 +327,7 @@
     backward(1, d1, 2, 5, g1, hand_on(d0, 1, s0, g0, 4))
     clear(d0, 1)
     rim_wait(4)
-    backward(0, d0, 2, 4, g0, last)
+    backward(0, d0, 1, 8, g0, last)
 
     def v_of(u):
         return (1 - half) * (7 - u) + half * u
@@ -390,8 +393,8 @@
     rg_out[...] = sum(rg[k, c] for k in range(5) for c in range(2))
 
     each_emb(lambda c: c.wait_send())
-    for k in range(layers):
-        w_copy(k).wait_send()
+    for k, a in every_w:
+        w_copy(k, a).wait_send()
     ro_copy.wait_send()
     each_cot(lambda c: c.wait_send())
     each_rg(lambda c: c.wait_send())
@@ -438,15 +441,15 @@
             pltpu.VMEM((2, 3, 3, 3, 256, 128), BF16),
             pltpu.VMEM((48, 128), F32),
             pltpu.VMEM((2, 8, 128), F32),
-            padded(23, 1), padded(24, 2), padded(24, 4),
+            padded(24, 1), padded(24, 2), padded(24, 4),
             padded(20, 4), padded(14, 2), padded(11, 1),
-            wide(21), wide(20), wide(15), wide(12), wide(10),
-            pltpu.VMEM((16, 64, 128), F32), pltpu.VMEM((15, Q, 16, 256), BF16),
+            wide(22), wide(20), wide(16), wide(12), wide(10),
+            pltpu.VMEM((16, 64, 128), F32), pltpu.VMEM((16, Q, 16, 256), BF16),
             pltpu.VMEM((2, 88, 128), F32),
             pltpu.VMEM((5, 2, 16, 128), F32),
             pltpu.VMEM((16, 128), F32),
             pltpu.VMEM((16, 128), F32),
-            dma((7, 2)), dma((7, 2)), dma((3,)), dma((3,)), dma((3,)),
+            dma((7, 2)), dma((7, 2)), dma((3,)), dma((3, 3)), dma((3, 3)),
             dma((2,)), dma((2,)), dma((1,)), dma((1,)),
             dma((5, 2)), dma((5, 2)), dma((1,)), dma((1,)),
             dma((5, 4)), dma((5, 4)),

time: 31 us -> 30.5 us (0.984)
  Pallas kernels: 30.1 us -> 29.6 us
    pallas_call x1, Pallas kernels: 28.2 us -> 27.7 us  [local(): pl.pallas_call(functools.partial(kernel, slabs), out_shape=out_shape, in_...]
where the time goes in v4:
time: 30.5 us; the launch traced here: 30.3 us
  Pallas kernels  29.6 us (97%)
  between operations  0.64 us (2%)
    pallas_call x1, Pallas kernels, local(): pl.pallas_call(functools.partial(kernel, slabs), out_shape=out_shape, in_...  27.7 us
    pallas_call x1, Pallas kernels, local(): pl.pallas_call(hand_out, out_shape=out_shape, in_specs=[anywhere] * 3, ou...  1.88 us

profile of v4, /device:TPU:9, one launch (start us, length us, event | category | flops | bytes accessed | tf_op | source)
XLA Modules:
  0.0 30.3 jit_solution(14482934605836345643)
XLA Ops:
  0.6 27.7 %shard_map.76 = (f32[16,64]{1,0:T(8,128)}, f32[16,128]{1,0:T(8,128)}, f32[16,128]{1,0:T(8,128)}) custom-call(bf16[16,128]{1,0:T(8,128)(2,1)} %left_ref.1, bf16[16,128]{1,0:T(8,128)(2,1)} %right_ref.1, bf16[3,3,3,256,128]{4,3,2,1,0:T(8,128)(2,1)} %w_hbm.1, f32[1,128]{1,0:T(1,128)} %bitcast.1, f32[16,64]{1,0:T(8,128)} %cot_ref.1), custom_call_target="tpu_custom_call" | custom-call | flops 8000000000 | bytes 4000000 | tf_op jit(solution)/shard_map/pallas_call | solution.py:432
  28.4 1.9 %shard_map.77 = (f32[16,64]{1,0:T(8,128)}, f32[16,128]{1,0:T(8,128)}, f32[16,128]{1,0:T(8,128)}) custom-call(f32[16,64]{1,0:T(8,128)} %get-tuple-element.6.refs_0_, f32[16,128]{1,0:T(8,128)} %get-tuple-element.7.refs_1_, f32[16,128]{1,0:T(8,128)} %get-tuple-element.8.refs_2_), custom_call_target="tpu_custom_call" | custom-call | tf_op jit(solution)/shard_map/pallas_call | solution.py:462

commit v5 on v4

--- a/solution.py
+++ b/solution.py
@@ -60,6 +60,11 @@
             src_ref=src, dst_ref=dst, send_sem=ss, recv_sem=rs,
             device_id=(slab + delta, chan), device_id_type=MESH,
         )
+
+    sign = 2 * half - 1
+
+    def bin_of(v):
+        return 7 + half + sign * v
 
     barrier = pltpu.get_barrier_semaphore()
     reach = max(BACK, AHEAD)
@@ -127,11 +132,35 @@
 
     ro_copy = send(ro.at[half], ro.at[half], ro_ss.at[0], ro_rs.at[0], 0, mate)
 
+    ro_copy.start()
+    each_cot(lambda c: c.start())
     each_emb(lambda c: c.start())
     for k, a in every_w:
         w_copy(k, a).start()
-    ro_copy.start()
-    each_cot(lambda c: c.start())
+    n_i = lax.broadcasted_iota(jnp.int32, (64, 128), 0)
+    d_i = lax.broadcasted_iota(jnp.int32, (64, 128), 1)
+    order = jnp.where(d_i == Q * (n_i % 16) + n_i // 16, 1.0, 0.0).astype(BF16)
+
+    send(ro.at[half], ro.at[mate], ro_ss.at[0], ro_rs.at[0], 0, mate).wait_recv()
+    for delta in (-1, 1):
+        @pl.when(there(delta))
+        def _(delta=delta):
+            slot = (1 + delta) // 2
+            send(
+                cot.at[pl.ds(16, 16)], cot.at[pl.ds(16 + 16 * delta, 16)],
+                cot_ss.at[slot], cot_rs.at[slot], delta, half,
+            ).wait_recv()
+    readout = jnp.concatenate([ro[0, 0:1], ro[1, 0:1]], axis=1)
+    parts = split3(readout)
+    row_i = lax.broadcasted_iota(jnp.int32, (16, 256), 0)
+    ro_rows = sum(
+        jnp.where(row_i == m, jnp.broadcast_to(part.astype(F32), (16, 256)), 0.0) for m, part in enumerate(parts)
+    ).astype(BF16)
+    cot_win = jnp.concatenate([cot[pl.ds(16 + bin_of(v), 1), :] for v in range(16)], axis=0)
+    cot_t = sum(nt(order, part) for part in split3(cot_win))
+
+    for v in range(16):
+        columns[v] = jnp.broadcast_to(cot_t[:, v : v + 1], (64, 128))
 
     def emb_wait(k, chan):
         send(block, emb.at[k, chan], emb_ss.at[k, chan], emb_rs.at[k, chan], 0, mate).wait_recv()
@@ -150,11 +179,6 @@
             rwin[c, 16 * k : 16 * k + 16] = emb[k, c, 0:16].astype(F32)
             if k < 3:
                 rwin[2 + c, 16 * k : 16 * k + 16] = emb[k, c, 16:32].astype(F32)
-
-    sign = 2 * half - 1
-
-    def bin_of(v):
-        return 7 + half + sign * v
 
     outer_edge = jnp.logical_or(
         jnp.logical_and(half == 0, slab == 0), jnp.logical_and(half == 1, slab == slabs - 1)
@@ -242,34 +266,12 @@
 
     forward(0, p0, 2, 11, keep(p1, 2, s0, 0))
     clear(p1, 2)
+    each_emb(lambda c: c.wait_send())
+    ro_copy.wait_send()
+    each_cot(lambda c: c.wait_send())
     rim_wait(0)
     forward(1, p1, 2, 10, keep(p2, 4, s1, 1))
     clear(p2, 4)
-
-    n_i = lax.broadcasted_iota(jnp.int32, (64, 128), 0)
-    d_i = lax.broadcasted_iota(jnp.int32, (64, 128), 1)
-    order = jnp.where(d_i == Q * (n_i % 16) + n_i // 16, 1.0, 0.0).astype(BF16)
-
-    send(ro.at[half], ro.at[mate], ro_ss.at[0], ro_rs.at[0], 0, mate).wait_recv()
-    for delta in (-1, 1):
-        @pl.when(there(delta))
-        def _(delta=delta):
-            slot = (1 + delta) // 2
-            send(
-                cot.at[pl.ds(16, 16)], cot.at[pl.ds(16 + 16 * delta, 16)],
-                cot_ss.at[slot], cot_rs.at[slot], delta, half,
-            ).wait_recv()
-    readout = jnp.concatenate([ro[0, 0:1], ro[1, 0:1]], axis=1)
-    parts = split3(readout)
-    row_i = lax.broadcasted_iota(jnp.int32, (16, 256), 0)
-    ro_rows = sum(
-        jnp.where(row_i == m, jnp.broadcast_to(part.astype(F32), (16, 256)), 0.0) for m, part in enumerate(parts)
-    ).astype(BF16)
-    cot_win = jnp.concatenate([cot[pl.ds(16 + bin_of(v), 1), :] for v in range(16)], axis=0)
-    cot_t = sum(nt(order, part) for part in split3(cot_win))
-
-    for v in range(16):
-        columns[v] = jnp.broadcast_to(cot_t[:, v : v + 1], (64, 128))
 
     def last_sink(index, begin, n, x, slope):
         column = columns[pl.ds(begin, n)]
@@ -283,14 +285,6 @@
     rim_wait(1)
     forward(2, p2, 2, 8, last_sink)
     clear(d2, 4)
-    contacts = [
-        jnp.sum(nt(ro_rows, p3[v].reshape(64, 256)), axis=0, keepdims=True) for v in range(8)
-    ]
-    outwards = jnp.concatenate(contacts, axis=0)
-    inwards = jnp.concatenate(contacts[::-1], axis=0)
-    contact_rows = jnp.where(half == 1, outwards, inwards)
-    contact = sum(jnp.dot(part, order, preferred_element_type=F32) for part in split3(contact_rows))
-
     def backward(k, src, steps, n, before, sink):
         r = 2**k
 
@@ -356,6 +350,14 @@
                         act(rg_copy(k, chan))
 
     each_rg(lambda c: c.start())
+    contacts = [
+        jnp.sum(nt(ro_rows, p3[v].reshape(64, 256)), axis=0, keepdims=True) for v in range(8)
+    ]
+    outwards = jnp.concatenate(contacts, axis=0)
+    inwards = jnp.concatenate(contacts[::-1], axis=0)
+    contact_rows = jnp.where(half == 1, outwards, inwards)
+    contact = sum(jnp.dot(part, order, preferred_element_type=F32) for part in split3(contact_rows))
+
     lg = jnp.concatenate(
         [jnp.sum(g0[v_of(u)].reshape(64, 256), axis=0, keepdims=True) for u in range(8)], axis=0
     )
@@ -375,6 +377,13 @@
         def _(k=k):
             rg[k] = jnp.zeros(rg.shape[1:], F32)
 
+    for k, a in every_w:
+        w_copy(k, a).wait_send()
+    for copies in rims:
+        for copy in copies:
+            copy.wait_send()
+    each_rg(lambda c: c.wait_send())
+    swap_copy.wait_send()
     swap_copy.wait_recv()
     lg_out[other, :] = swap[0:8]
     contact_out[other, :] = swap[8:16, :64]
@@ -391,17 +400,6 @@
                 for chan in range(2):
                     rg_wait(k, chan)
     rg_out[...] = sum(rg[k, c] for k in range(5) for c in range(2))
-
-    each_emb(lambda c: c.wait_send())
-    for k, a in every_w:
-        w_copy(k, a).wait_send()
-    ro_copy.wait_send()
-    each_cot(lambda c: c.wait_send())
-    each_rg(lambda c: c.wait_send())
-    swap_copy.wait_send()
-    for copies in rims:
-        for copy in copies:
-            copy.wait_send()
 
 
 def hand_out(*refs):

time: 30.5 us -> 30.3 us (level)
  no operation moved by 1% of the time
where the time goes in v5:
time: 30.3 us; the launch traced here: 30.1 us
  Pallas kernels  29.5 us (97%)
  between operations  0.64 us (2%)
    pallas_call x1, Pallas kernels, local(): pl.pallas_call(functools.partial(kernel, slabs), out_shape=out_shape, in_...  27.6 us
    pallas_call x1, Pallas kernels, local(): pl.pallas_call(hand_out, out_shape=out_shape, in_specs=[anywhere] * 3, ou...  1.88 us

profile of v5, /device:TPU:9, one launch (start us, length us, event | category | flops | bytes accessed | tf_op | source)
XLA Modules:
  0.0 30.1 jit_solution(4901377131134838337)
XLA Ops:
  0.6 27.6 %shard_map.76 = (f32[16,64]{1,0:T(8,128)}, f32[16,128]{1,0:T(8,128)}, f32[16,128]{1,0:T(8,128)}) custom-call(bf16[16,128]{1,0:T(8,128)(2,1)} %left_ref.1, bf16[16,128]{1,0:T(8,128)(2,1)} %right_ref.1, bf16[3,3,3,256,128]{4,3,2,1,0:T(8,128)(2,1)} %w_hbm.1, f32[1,128]{1,0:T(1,128)} %bitcast.1, f32[16,64]{1,0:T(8,128)} %cot_ref.1), custom_call_target="tpu_custom_call" | custom-call | flops 8000000000 | bytes 4000000 | tf_op jit(solution)/shard_map/pallas_call | solution.py:430
  28.2 1.9 %shard_map.77 = (f32[16,64]{1,0:T(8,128)}, f32[16,128]{1,0:T(8,128)}, f32[16,128]{1,0:T(8,128)}) custom-call(f32[16,64]{1,0:T(8,128)} %get-tuple-element.6.refs_0_, f32[16,128]{1,0:T(8,128)} %get-tuple-element.7.refs_1_, f32[16,128]{1,0:T(8,128)} %get-tuple-element.8.refs_2_), custom_call_target="tpu_custom_call" | custom-call | tf_op jit(solution)/shard_map/pallas_call | solution.py:460

commit v6 on v5

--- a/solution.py
+++ b/solution.py
@@ -114,8 +114,12 @@
                     for chan in range(2):
                         act(emb_copy(delta, chan))
 
+    distances = {(1, 1): 1, (2, 1): 1, (1, 2): 2, (2, 2): 2, (2, 0): 4} if slabs % 8 == 0 else {}
+
     def w_copy(k, a):
-        return send(w_hbm.at[k, a], w.at[half, k, a], w_ss.at[k, a], w_rs.at[k, a], 0, mate)
+        far = distances.get((k, a), 0)
+        delta = far - 2 * far * (slab // far % 2) if far else 0
+        return send(w_hbm.at[k, a], w.at[half, k, a], w_ss.at[k, a], w_rs.at[k, a], delta, mate)
 
     every_w = [(k, a) for k in range(layers) for a in range(3)]
 
@@ -135,7 +139,7 @@
     ro_copy.start()
     each_cot(lambda c: c.start())
     each_emb(lambda c: c.start())
-    for k, a in every_w:
+    for k, a in sorted(every_w, key=lambda piece: distances.get(piece, 0) == 0):
         w_copy(k, a).start()
     n_i = lax.broadcasted_iota(jnp.int32, (64, 128), 0)
     d_i = lax.broadcasted_iota(jnp.int32, (64, 128), 1)

time: 30.3 us -> 31 us (1.023)
  Pallas kernels: 29.5 us -> 29.9 us
    pallas_call x1, Pallas kernels: 27.6 us -> 28 us  [local(): pl.pallas_call(functools.partial(kernel, slabs), out_shape=out_shape, in_...]
where the time goes in v6:
time: 31 us; the launch traced here: 30.6 us
  Pallas kernels  29.9 us (96%)
  between operations  0.64 us (2%)
    pallas_call x1, Pallas kernels, local(): pl.pallas_call(functools.partial(kernel, slabs), out_shape=out_shape, in_...  28 us
    pallas_call x1, Pallas kernels, local(): pl.pallas_call(hand_out, out_shape=out_shape, in_specs=[anywhere] * 3, ou...  1.88 us

profile of v6, /device:TPU:9, one launch (start us, length us, event | category | flops | bytes accessed | tf_op | source)
XLA Modules:
  0.0 30.6 jit_solution(94511999815363745)
XLA Ops:
  0.6 28.0 %shard_map.76 = (f32[16,64]{1,0:T(8,128)}, f32[16,128]{1,0:T(8,128)}, f32[16,128]{1,0:T(8,128)}) custom-call(bf16[16,128]{1,0:T(8,128)(2,1)} %left_ref.1, bf16[16,128]{1,0:T(8,128)(2,1)} %right_ref.1, bf16[3,3,3,256,128]{4,3,2,1,0:T(8,128)(2,1)} %w_hbm.1, f32[1,128]{1,0:T(1,128)} %bitcast.1, f32[16,64]{1,0:T(8,128)} %cot_ref.1), custom_call_target="tpu_custom_call" | custom-call | flops 8000000000 | bytes 4000000 | tf_op jit(solution)/shard_map/pallas_call | solution.py:434
  28.7 1.9 %shard_map.77 = (f32[16,64]{1,0:T(8,128)}, f32[16,128]{1,0:T(8,128)}, f32[16,128]{1,0:T(8,128)}) custom-call(f32[16,64]{1,0:T(8,128)} %get-tuple-element.6.refs_0_, f32[16,128]{1,0:T(8,128)} %get-tuple-element.7.refs_1_, f32[16,128]{1,0:T(8,128)} %get-tuple-element.8.refs_2_), custom_call_target="tpu_custom_call" | custom-call | tf_op jit(solution)/shard_map/pallas_call | solution.py:464

commit v7 on v5

--- a/solution.py
+++ b/solution.py
@@ -44,7 +44,7 @@
     slabs,
     left_ref, right_ref, w_hbm, ro_ref, cot_ref,
     contact_out, lg_out, rg_out,
-    block, emb, rwin, w, cot, ro, p0, p1, p2, d2, d1, d0, s0, s1, g2, g1, g0, columns, p3,
+    block, emb, rwin, w, wt, cot, ro, p0, p1, p2, d2, d1, d0, s0, s1, g2, g1, g0, columns, p3,
     spread, rg, swap_out, swap,
     emb_ss, emb_rs, w_ls, w_ss, w_rs, cot_ss, cot_rs, ro_ss, ro_rs, rg_ss, rg_rs, swap_ss, swap_rs, rim_ss, rim_rs,
 ):
@@ -162,6 +162,17 @@
     for v in range(16):
         columns[v] = jnp.broadcast_to(cot_t[:, v : v + 1], (64, 128))
 
+    def turn(k, chan):
+        def one(tap, unused):
+            wt[chan, k, tap // 3, tap % 3] = w[chan, k, tap // 3, tap % 3].T
+            return unused
+
+        lax.fori_loop(0, 9, one, 0)
+
+    for k in range(layers):
+        local[k].wait()
+        turn(k, half)
+
     def emb_wait(k, chan):
         send(block, emb.at[k, chan], emb_ss.at[k, chan], emb_rs.at[k, chan], 0, mate).wait_recv()
 
@@ -221,7 +232,6 @@
     taps = [2 - 2 * half, 1, 2 * half]
 
     def weights(k):
-        local[k].wait()
         for a in range(3):
             send(w_hbm.at[k, a], w.at[mate, k, a], w_ss.at[k, a], w_rs.at[k, a], 0, mate).wait_recv()
 
@@ -269,6 +279,7 @@
     each_emb(lambda c: c.wait_send())
     ro_copy.wait_send()
     each_cot(lambda c: c.wait_send())
+    turn(0, mate)
     rim_wait(0)
     forward(1, p1, 2, 10, keep(p2, 4, s1, 1))
     clear(p2, 4)
@@ -282,6 +293,7 @@
         g2[pl.ds(begin, n)] = grad
         p3[pl.ds(begin, n)] = x.astype(BF16)
 
+    turn(1, mate)
     rim_wait(1)
     forward(2, p2, 2, 8, last_sink)
     clear(d2, 4)
@@ -290,7 +302,7 @@
 
         def step(index, unused):
             begin = index * n
-            wide = jnp.concatenate([w[c, k, a, b] for a in taps for b in range(3) for c in range(2)], axis=1)
+            wide = jnp.concatenate([wt[c, k, a, b] for a in taps for b in range(3) for c in range(2)], axis=0)
             lhs = jnp.concatenate(
                 [
                     src[pl.ds(begin + (2 - m) * r, n), (2 - b) * r : (2 - b) * r + Q].reshape(n * 64, 256)
@@ -298,7 +310,8 @@
                 ],
                 axis=1,
             )
-            sink(index, begin, n, before[pl.ds(begin, n)] + nt(lhs, wide).reshape(n, Q, 16, 256))
+            sink(index, begin, n, before[pl.ds(begin, n)]
+                 + jnp.dot(lhs, wide, preferred_element_type=F32).reshape(n, Q, 16, 256))
             return unused
 
         lax.fori_loop(0, steps, step, 0)
@@ -314,6 +327,7 @@
     def last(index, begin, n, grad):
         g0[pl.ds(begin, n)] = grad
 
+    turn(2, mate)
     rim_wait(2)
     backward(2, d2, 2, 6, g2, hand_on(d1, 2, s1, g1, 3))
     clear(d1, 2)
@@ -437,6 +451,7 @@
             pltpu.VMEM((7, 2, 32, 128), BF16),
             pltpu.VMEM((4, 112, 128), F32),
             pltpu.VMEM((2, 3, 3, 3, 256, 128), BF16),
+            pltpu.VMEM((2, 3, 3, 3, 128, 256), BF16),
             pltpu.VMEM((48, 128), F32),
             pltpu.VMEM((2, 8, 128), F32),
             padded(24, 1), padded(24, 2), padded(24, 4),

time: 30.3 us -> 32 us (1.056)
  Pallas kernels: 29.5 us -> 31.1 us
    pallas_call x1, Pallas kernels: 27.6 us -> 29.2 us  [local(): pl.pallas_call(functools.partial(kernel, slabs), out_shape=out_shape, in_...]
where the time goes in v7:
time: 32 us; the launch traced here: 31.7 us
  Pallas kernels  31.1 us (97%)
  between operations  0.64 us (2%)
    pallas_call x1, Pallas kernels, local(): pl.pallas_call(functools.partial(kernel, slabs), out_shape=out_shape, in_...  29.2 us
    pallas_call x1, Pallas kernels, local(): pl.pallas_call(hand_out, out_shape=out_shape, in_specs=[anywhere] * 3, ou...  1.88 us

profile of v7, /device:TPU:9, one launch (start us, length us, event | category | flops | bytes accessed | tf_op | source)
XLA Modules:
  0.0 31.7 jit_solution(15762873567372894881)
XLA Ops:
  0.6 29.2 %shard_map.76 = (f32[16,64]{1,0:T(8,128)}, f32[16,128]{1,0:T(8,128)}, f32[16,128]{1,0:T(8,128)}) custom-call(bf16[16,128]{1,0:T(8,128)(2,1)} %left_ref.1, bf16[16,128]{1,0:T(8,128)(2,1)} %right_ref.1, bf16[3,3,3,256,128]{4,3,2,1,0:T(8,128)(2,1)} %w_hbm.1, f32[1,128]{1,0:T(1,128)} %bitcast.1, f32[16,64]{1,0:T(8,128)} %cot_ref.1), custom_call_target="tpu_custom_call" | custom-call | flops 8000000000 | bytes 4000000 | tf_op jit(solution)/shard_map/pallas_call | solution.py:444
  29.9 1.9 %shard_map.77 = (f32[16,64]{1,0:T(8,128)}, f32[16,128]{1,0:T(8,128)}, f32[16,128]{1,0:T(8,128)}) custom-call(f32[16,64]{1,0:T(8,128)} %get-tuple-element.6.refs_0_, f32[16,128]{1,0:T(8,128)} %get-tuple-element.7.refs_1_, f32[16,128]{1,0:T(8,128)} %get-tuple-element.8.refs_2_), custom_call_target="tpu_custom_call" | custom-call | tf_op jit(solution)/shard_map/pallas_call | solution.py:475

commit v8 on v5

--- a/solution.py
+++ b/solution.py
@@ -242,7 +242,9 @@
                 ],
                 axis=1,
             )
-            z = jnp.dot(lhs, wide, preferred_element_type=F32).reshape(n, Q, 16, 256)
+            z = sum(
+                jnp.dot(lhs[:, m : m + 768], wide[m : m + 768], preferred_element_type=F32) for m in (0, 768, 1536)
+            ).reshape(n, Q, 16, 256)
             s = 0.5 + 0.5 * jnp.tanh(0.5 * z)
             old = src[pl.ds(begin + r, n), r : r + Q].astype(F32)
             zs = z * s
@@ -298,7 +300,9 @@
                 ],
                 axis=1,
             )
-            sink(index, begin, n, before[pl.ds(begin, n)] + nt(lhs, wide).reshape(n, Q, 16, 256))
+            sink(index, begin, n, before[pl.ds(begin, n)] + sum(
+                nt(lhs[:, m : m + 768], wide[:, m : m + 768]) for m in (0, 768, 1536)
+            ).reshape(n, Q, 16, 256))
             return unused
 
         lax.fori_loop(0, steps, step, 0)

time: 30.3 us -> 30.3 us (level)
  no operation moved by 1% of the time
where the time goes in v8:
time: 30.3 us; the launch traced here: 30.1 us
  Pallas kernels  29.4 us (97%)
  between operations  0.64 us (2%)
    pallas_call x1, Pallas kernels, local(): pl.pallas_call(functools.partial(kernel, slabs), out_shape=out_shape, in_...  27.6 us
    pallas_call x1, Pallas kernels, local(): pl.pallas_call(hand_out, out_shape=out_shape, in_specs=[anywhere] * 3, ou...  1.88 us

profile of v8, /device:TPU:9, one launch (start us, length us, event | category | flops | bytes accessed | tf_op | source)
XLA Modules:
  0.0 30.1 jit_solution(7159224932795635383)
XLA Ops:
  0.6 27.6 %shard_map.76 = (f32[16,64]{1,0:T(8,128)}, f32[16,128]{1,0:T(8,128)}, f32[16,128]{1,0:T(8,128)}) custom-call(bf16[16,128]{1,0:T(8,128)(2,1)} %left_ref.1, bf16[16,128]{1,0:T(8,128)(2,1)} %right_ref.1, bf16[3,3,3,256,128]{4,3,2,1,0:T(8,128)(2,1)} %w_hbm.1, f32[1,128]{1,0:T(1,128)} %bitcast.1, f32[16,64]{1,0:T(8,128)} %cot_ref.1), custom_call_target="tpu_custom_call" | custom-call | flops 8000000000 | bytes 4000000 | tf_op jit(solution)/shard_map/pallas_call | solution.py:434
  28.2 1.9 %shard_map.77 = (f32[16,64]{1,0:T(8,128)}, f32[16,128]{1,0:T(8,128)}, f32[16,128]{1,0:T(8,128)}) custom-call(f32[16,64]{1,0:T(8,128)} %get-tuple-element.6.refs_0_, f32[16,128]{1,0:T(8,128)} %get-tuple-element.7.refs_1_, f32[16,128]{1,0:T(8,128)} %get-tuple-element.8.refs_2_), custom_call_target="tpu_custom_call" | custom-call | tf_op jit(solution)/shard_map/pallas_call | solution.py:464
